TPU v7x, 128 devices: a whole 4x4x4 slice. The times are simulated.
128 devices in a mesh: grp: 4 (over x), sub: 32 (over y, z, core).
Axes of the slice: x: 4, y: 4, z: 4, core: 2. Of those that a mesh axis runs over, the one named last changes fastest.
Arguments:
- coordinates: bfloat16 [8192, 3, 256], P(('grp', 'sub')), may hold values from -1 to 1
- charges: bfloat16 [8192, 16, 256], P(('grp', 'sub')), may hold values from -6 to 6
- leaf_basis: bfloat16 [8192, 64, 256], P(('grp', 'sub')), may hold values from -0.375 to 0.375
- transfer: bfloat16 [8192, 64, 64], P(('grp', 'sub')), may hold values from -0.75 to 0.75
- skeleton: bfloat16 [1024, 3, 64], P(('grp', 'sub')), may hold values from -1 to 1
- send_plan: int32 [128, 128, 4], P(('grp', 'sub')), may hold values from 0 to 63
- near_lists: int32 [8192, 16], P(('grp', 'sub')), may hold values from 0 to 575
- near_count: int32 [8192], P(('grp', 'sub')), may hold values from 1 to 16, as said below
- far_lists: int32 [1024, 27], P(('grp', 'sub')), may hold values from 0 to 1023
Outputs:
- potential: bfloat16 [8192, 16, 256], P(('grp', 'sub'))
Inputs may be any that keep to these rules, and one draw needn't show every extreme that they name: Entries of a leaf's neighbour list at positions near_count or later are ignored. Each device's leaves carry their own largest count; some device's largest is 16.
All inputs are finite; a program needn't handle non-finite values.
Results may differ from a plain program's by a relative error of at most 0.024.
Values may be sent and summed in bfloat16 or wider, within the bound.
No kernel may reach another device: no remote copies, remote signals or barrier semaphores. Data moves between devices by JAX's collectives and lax.ppermute only.
A program may use at most 64 MiB of HBM per device.

v0:
```python
import jax
import jax.numpy as jnp
from jax import lax
from jax.sharding import PartitionSpec as P

SOFTENING = 0.01


def kernel_block(targets, sources):
    target_pos = targets.astype(jnp.float32)
    source_pos = sources.astype(jnp.float32)
    squared = jnp.zeros(
        source_pos.shape[:-2] + (source_pos.shape[-1], target_pos.shape[-1]), jnp.float32
    )
    for component in range(3):
        offset = source_pos[..., component, :, None] - target_pos[..., component, None, :]
        squared = squared + offset * offset
    return lax.rsqrt(squared + SOFTENING).astype(jnp.bfloat16)


def body(
    coordinates,
    charges,
    leaf_basis,
    transfer,
    skeleton,
    send_plan,
    near_lists,
    near_count,
    far_lists,
):
    leaf_dev, rhs_count, points = charges.shape
    basis_rank = leaf_basis.shape[1]
    list_length = near_lists.shape[1]
    far_length = far_lists.shape[1]
    moments = jnp.einsum(
        "lkp,lrp->lrk", leaf_basis, charges, preferred_element_type=jnp.float32
    ).astype(jnp.bfloat16)
    lifted = jnp.einsum("lrk,lkj->lrj", moments, transfer, preferred_element_type=jnp.float32)
    parent_moments = (
        lifted.reshape(leaf_dev // 8, 8, rhs_count, basis_rank).sum(axis=1).astype(jnp.bfloat16)
    )
    all_moments, all_skeleton = (
        lax.all_gather(parent_moments, ("grp", "sub"), axis=0, tiled=True),
        lax.all_gather(skeleton, ("grp", "sub"), axis=0, tiled=True),
    )
    send_rows = send_plan[0]
    out_coords = coordinates[send_rows]
    out_charges = charges[send_rows]
    ghost_coords, ghost_charges = (
        lax.all_to_all(out_coords, ("grp", "sub"), split_axis=0, concat_axis=0, tiled=True),
        lax.all_to_all(out_charges, ("grp", "sub"), split_axis=0, concat_axis=0, tiled=True),
    )
    table_coords = jnp.concatenate(
        [coordinates, ghost_coords.reshape((-1,) + coordinates.shape[1:])], axis=0
    )
    table_charges = jnp.concatenate(
        [charges, ghost_charges.reshape((-1,) + charges.shape[1:])], axis=0
    )
    own_kernel = kernel_block(coordinates, coordinates)
    start_sum = jnp.einsum("lrs,lst->lrt", charges, own_kernel, preferred_element_type=jnp.float32)

    def near_step(column, total):
        slot_index = lax.dynamic_index_in_dim(near_lists, column, axis=1, keepdims=False)
        kernel_vals = kernel_block(coordinates, table_coords[slot_index])
        block_term = jnp.einsum(
            "lrs,lst->lrt",
            table_charges[slot_index],
            kernel_vals,
            preferred_element_type=jnp.float32,
        )
        is_live = (column < near_count)[:, None, None]
        return total + jnp.where(is_live, block_term, jnp.float32(0.0))

    last_column = jnp.int32(list_length)
    near_sum = lax.fori_loop(jnp.int32(0), last_column, near_step, start_sum)
    near_sum = float(points * (list_length + 1)) ** (-0.5) * near_sum
    far_moments = all_moments[far_lists]
    far_skeleton = all_skeleton[far_lists]
    couple = kernel_block(skeleton[:, None], far_skeleton)
    far_scale = float(far_length * basis_rank) ** (-0.5)
    local_coef = (
        far_scale
        * jnp.einsum("pfrs,pfst->prt", far_moments, couple, preferred_element_type=jnp.float32)
    ).astype(jnp.bfloat16)
    parent_of = jnp.arange(leaf_dev, dtype=jnp.int32) // 8
    child_coef = jnp.einsum(
        "lrj,lkj->lrk", local_coef[parent_of], transfer, preferred_element_type=jnp.float32
    ).astype(jnp.bfloat16)
    far_field = jnp.einsum(
        "lrk,lkp->lrp", child_coef, leaf_basis, preferred_element_type=jnp.float32
    )
    return (near_sum + far_field).astype(jnp.bfloat16)


def solution(mesh):
    in_specs = (
        P(("grp", "sub"), None, None),
        P(("grp", "sub"), None, None),
        P(("grp", "sub"), None, None),
        P(("grp", "sub"), None, None),
        P(("grp", "sub"), None, None),
        P(("grp", "sub"), None, None),
        P(("grp", "sub"), None),
        P(("grp", "sub")),
        P(("grp", "sub"), None),
    )
    out_specs = P(("grp", "sub"), None, None)
    return jax.shard_map(body, mesh=mesh, in_specs=in_specs, out_specs=out_specs, check_vma=False)
```

profile of v0, /device:TPU:1, one launch (start us, length us, event | category | flops | bytes accessed | tf_op | source)
XLA Modules:
  0.0 456.5 jit_solution(3506796237583363786)
XLA Ops:
  7.6 3.7 gather_fusion.3
  14.7 11.5 %all-to-all-start.1 = ((bf16[128,4,3,256]{3,1,2,0:T(4,128)(2,1)}), bf16[128,4,3,256]{3,1,2,0:T(4,128)(2,1)S(1)}, u32[]{:S(2)}, u32[]{:S(2)}) async-start(bf16[128,4,3,256]{3,1,2,0:T(4,128)(2,1)} %copy.29), calls=%async_computation.1 | async-start | bytes 1572864 | tf_op jit(solution)/shard_map/all_to_all | solution.py:51
  29.1 3.5 gather_fusion.2
  32.6 10.1 %all-to-all-done.1 = bf16[128,4,3,256]{3,1,2,0:T(4,128)(2,1)S(1)} async-done(((bf16[128,4,3,256]{3,1,2,0:T(4,128)(2,1)}), bf16[128,4,3,256]{3,1,2,0:T(4,128)(2,1)S(1)}, u32[]{:S(2)}, u32[]{:S(2)}) %all-to-all-start.1) | async-done | bytes 786464 | tf_op jit(solution)/shard_map/all_to_all | solution.py:51
  42.7 5.7 %all-to-all-start = ((bf16[128,4,16,256]{3,2,1,0:T(8,128)(2,1)}), bf16[128,4,16,256]{3,2,1,0:T(8,128)(2,1)}, u32[]{:S(2)}, u32[]{:S(2)}) async-start(bf16[128,4,16,256]{3,2,1,0:T(8,128)(2,1)} %bitcast.78), calls=%async_computation | async-start | bytes 8388608 | tf_op jit(solution)/shard_map/all_to_all | solution.py:52
  49.2 79.3 %all_gather.7 = bf16[1024,3,64]{2,0,1:T(8,128)(2,1)S(1)} all-gather(bf16[8,3,64]{2,0,1:T(8,128)(2,1)S(1)} %copy-done.3), channel_id=1, replica_groups=mesh['grp'=4,'sub'=32] {'grp','sub'}, dimensions={0}, use_global_device_ids=true | all-gather | bytes 396288 | tf_op jit(solution)/shard_map/all_gather | solution.py:45
  141.0 10.3 %fusion.7 = f32[64,16,256]{2,1,0:T(8,128)} fusion(bf16[64,16,256]{2,1,0:T(8,128)(2,1)S(1)} %copy-done.2, f32[64,256]{1,0:T(8,128)S(1)} %get-tuple-element.84, f32[64,256]{1,0:T(8,128)S(1)} %get-tuple-element.85, f32[64,256]{1,0:T(8,128)S(1)} %get-tuple-element.83), kind=kOutput, calls=%fused_computation.28 | convolution fusion | flops 176160768 | bytes 1769472 | tf_op jit(solution)/shard_map/lrs,lst->lrt/dot_general | solution.py:61
  155.8 3.9 gather_fusion.4
  159.7 8.1 %fusion.12 = bf16[8,16,64]{2,1,0:T(8,128)(2,1)S(1)} fusion(bf16[8,27,16,64]{3,2,1,0:T(8,128)(2,1)} %bitcast.79, f32[8,64]{1,0:T(8,128)S(1)} %get-tuple-element.87, f32[8,27,64]{2,1,0:T(8,128)} %get-tuple-element.81, f32[8,64]{1,0:T(8,128)S(1)} %get-tuple-element.88, f32[8,27,64]{2,1,0:T(8,128)} %get-tuple-element.82, f32[8,64]{1,0:T(8,128)S(1)} %get-tuple-element.86, ...), kind=kOutput, calls=%fused_computation.35 | convolution fusion | flops 37175296 | bytes 630784 | tf_op jit(solution)/shard_map/pfrs,pfst->prt/dot_general | solution.py:84
  168.5 4.8 %pad_maximum_fusion = bf16[576,16,256]{2,1,0:T(8,128)(2,1)} fusion(bf16[512,16,256]{2,1,0:T(8,128)(2,1)} %bitcast.10, bf16[64,16,256]{2,1,0:T(8,128)(2,1)S(1)} %copy-done.2), kind=kLoop, calls=%fused_computation.25 | loop fusion | flops 2359296 | bytes 9437184 | tf_op jit(solution)/shard_map/concatenate | solution.py:57
  173.3 273.0 %while.10 = (s32[]{:T(128)}, f32[64,16,256]{2,1,0:T(8,128)}, s32[64]{0:T(128)S(1)}, s32[64,16]{0,1:T(8,128)}, bf16[576,16,256]{2,1,0:T(8,128)(2,1)}, /*index=5*/...) while((s32[]{:T(128)}, f32[64,16,256]{2,1,0:T(8,128)}, s32[64]{0:T(128)S(1)}, ...), condition=%wide.region_1.2_spmd, body=%wide.region_0.0_spmd.sunk | while | flops 176735488 | bytes 5740253 | solution.py:76
  176.2 2.9 gather_fusion
  179.2 11.2 %fusion.33 = f32[64,16,256]{2,1,0:T(8,128)} fusion(f32[64,16,256]{2,1,0:T(8,128)} %get-tuple-element.159, bf16[64,16,256]{2,1,0:T(8,128)(2,1)S(1)} %gather_fusion, f32[64,256]{1,0:T(8,128)S(1)} %get-tuple-element.142, f32[64,256]{1,0:T(8,128)S(1)} %get-tuple-element.145, f32[64,256]{1,0:T(8,128)S(1)} %get-tuple-element.146, ...), kind=kOutput, calls=%fused_computation.10.clone.1 | convolution fusion | flops 176685056 | bytes 3014720 | tf_op jit(solution)/shard_map/while/body/lrs,lst->lrt/dot_general | solution.py:66
  193.3 2.9 gather_fusion
  196.2 11.2 %fusion.33 = f32[64,16,256]{2,1,0:T(8,128)} fusion(f32[64,16,256]{2,1,0:T(8,128)} %get-tuple-element.159, bf16[64,16,256]{2,1,0:T(8,128)(2,1)S(1)} %gather_fusion, f32[64,256]{1,0:T(8,128)S(1)} %get-tuple-element.142, f32[64,256]{1,0:T(8,128)S(1)} %get-tuple-element.145, f32[64,256]{1,0:T(8,128)S(1)} %get-tuple-element.146, ...), kind=kOutput, calls=%fused_computation.10.clone.1 | convolution fusion | flops 176685056 | bytes 3014720 | tf_op jit(solution)/shard_map/while/body/lrs,lst->lrt/dot_general | solution.py:66
  213.3 11.2 %fusion.33 = f32[64,16,256]{2,1,0:T(8,128)} fusion(f32[64,16,256]{2,1,0:T(8,128)} %get-tuple-element.159, bf16[64,16,256]{2,1,0:T(8,128)(2,1)S(1)} %gather_fusion, f32[64,256]{1,0:T(8,128)S(1)} %get-tuple-element.142, f32[64,256]{1,0:T(8,128)S(1)} %get-tuple-element.145, f32[64,256]{1,0:T(8,128)S(1)} %get-tuple-element.146, ...), kind=kOutput, calls=%fused_computation.10.clone.1 | convolution fusion | flops 176685056 | bytes 3014720 | tf_op jit(solution)/shard_map/while/body/lrs,lst->lrt/dot_general | solution.py:66
  227.4 2.9 gather_fusion
  230.4 11.2 %fusion.33 = f32[64,16,256]{2,1,0:T(8,128)} fusion(f32[64,16,256]{2,1,0:T(8,128)} %get-tuple-element.159, bf16[64,16,256]{2,1,0:T(8,128)(2,1)S(1)} %gather_fusion, f32[64,256]{1,0:T(8,128)S(1)} %get-tuple-element.142, f32[64,256]{1,0:T(8,128)S(1)} %get-tuple-element.145, f32[64,256]{1,0:T(8,128)S(1)} %get-tuple-element.146, ...), kind=kOutput, calls=%fused_computation.10.clone.1 | convolution fusion | flops 176685056 | bytes 3014720 | tf_op jit(solution)/shard_map/while/body/lrs,lst->lrt/dot_general | solution.py:66
  244.5 2.9 gather_fusion
  247.4 11.2 %fusion.33 = f32[64,16,256]{2,1,0:T(8,128)} fusion(f32[64,16,256]{2,1,0:T(8,128)} %get-tuple-element.159, bf16[64,16,256]{2,1,0:T(8,128)(2,1)S(1)} %gather_fusion, f32[64,256]{1,0:T(8,128)S(1)} %get-tuple-element.142, f32[64,256]{1,0:T(8,128)S(1)} %get-tuple-element.145, f32[64,256]{1,0:T(8,128)S(1)} %get-tuple-element.146, ...), kind=kOutput, calls=%fused_computation.10.clone.1 | convolution fusion | flops 176685056 | bytes 3014720 | tf_op jit(solution)/shard_map/while/body/lrs,lst->lrt/dot_general | solution.py:66
  264.5 11.2 %fusion.33 = f32[64,16,256]{2,1,0:T(8,128)} fusion(f32[64,16,256]{2,1,0:T(8,128)} %get-tuple-element.159, bf16[64,16,256]{2,1,0:T(8,128)(2,1)S(1)} %gather_fusion, f32[64,256]{1,0:T(8,128)S(1)} %get-tuple-element.142, f32[64,256]{1,0:T(8,128)S(1)} %get-tuple-element.145, f32[64,256]{1,0:T(8,128)S(1)} %get-tuple-element.146, ...), kind=kOutput, calls=%fused_computation.10.clone.1 | convolution fusion | flops 176685056 | bytes 3014720 | tf_op jit(solution)/shard_map/while/body/lrs,lst->lrt/dot_general | solution.py:66
  281.6 11.2 %fusion.33 = f32[64,16,256]{2,1,0:T(8,128)} fusion(f32[64,16,256]{2,1,0:T(8,128)} %get-tuple-element.159, bf16[64,16,256]{2,1,0:T(8,128)(2,1)S(1)} %gather_fusion, f32[64,256]{1,0:T(8,128)S(1)} %get-tuple-element.142, f32[64,256]{1,0:T(8,128)S(1)} %get-tuple-element.145, f32[64,256]{1,0:T(8,128)S(1)} %get-tuple-element.146, ...), kind=kOutput, calls=%fused_computation.10.clone.1 | convolution fusion | flops 176685056 | bytes 3014720 | tf_op jit(solution)/shard_map/while/body/lrs,lst->lrt/dot_general | solution.py:66
  298.6 11.2 %fusion.33 = f32[64,16,256]{2,1,0:T(8,128)} fusion(f32[64,16,256]{2,1,0:T(8,128)} %get-tuple-element.159, bf16[64,16,256]{2,1,0:T(8,128)(2,1)S(1)} %gather_fusion, f32[64,256]{1,0:T(8,128)S(1)} %get-tuple-element.142, f32[64,256]{1,0:T(8,128)S(1)} %get-tuple-element.145, f32[64,256]{1,0:T(8,128)S(1)} %get-tuple-element.146, ...), kind=kOutput, calls=%fused_computation.10.clone.1 | convolution fusion | flops 176685056 | bytes 3014720 | tf_op jit(solution)/shard_map/while/body/lrs,lst->lrt/dot_general | solution.py:66
  315.7 11.2 %fusion.33 = f32[64,16,256]{2,1,0:T(8,128)} fusion(f32[64,16,256]{2,1,0:T(8,128)} %get-tuple-element.159, bf16[64,16,256]{2,1,0:T(8,128)(2,1)S(1)} %gather_fusion, f32[64,256]{1,0:T(8,128)S(1)} %get-tuple-element.142, f32[64,256]{1,0:T(8,128)S(1)} %get-tuple-element.145, f32[64,256]{1,0:T(8,128)S(1)} %get-tuple-element.146, ...), kind=kOutput, calls=%fused_computation.10.clone.1 | convolution fusion | flops 176685056 | bytes 3014720 | tf_op jit(solution)/shard_map/while/body/lrs,lst->lrt/dot_general | solution.py:66
  332.8 11.2 %fusion.33 = f32[64,16,256]{2,1,0:T(8,128)} fusion(f32[64,16,256]{2,1,0:T(8,128)} %get-tuple-element.159, bf16[64,16,256]{2,1,0:T(8,128)(2,1)S(1)} %gather_fusion, f32[64,256]{1,0:T(8,128)S(1)} %get-tuple-element.142, f32[64,256]{1,0:T(8,128)S(1)} %get-tuple-element.145, f32[64,256]{1,0:T(8,128)S(1)} %get-tuple-element.146, ...), kind=kOutput, calls=%fused_computation.10.clone.1 | convolution fusion | flops 176685056 | bytes 3014720 | tf_op jit(solution)/shard_map/while/body/lrs,lst->lrt/dot_general | solution.py:66
  349.8 11.2 %fusion.33 = f32[64,16,256]{2,1,0:T(8,128)} fusion(f32[64,16,256]{2,1,0:T(8,128)} %get-tuple-element.159, bf16[64,16,256]{2,1,0:T(8,128)(2,1)S(1)} %gather_fusion, f32[64,256]{1,0:T(8,128)S(1)} %get-tuple-element.142, f32[64,256]{1,0:T(8,128)S(1)} %get-tuple-element.145, f32[64,256]{1,0:T(8,128)S(1)} %get-tuple-element.146, ...), kind=kOutput, calls=%fused_computation.10.clone.1 | convolution fusion | flops 176685056 | bytes 3014720 | tf_op jit(solution)/shard_map/while/body/lrs,lst->lrt/dot_general | solution.py:66
  366.9 11.2 %fusion.33 = f32[64,16,256]{2,1,0:T(8,128)} fusion(f32[64,16,256]{2,1,0:T(8,128)} %get-tuple-element.159, bf16[64,16,256]{2,1,0:T(8,128)(2,1)S(1)} %gather_fusion, f32[64,256]{1,0:T(8,128)S(1)} %get-tuple-element.142, f32[64,256]{1,0:T(8,128)S(1)} %get-tuple-element.145, f32[64,256]{1,0:T(8,128)S(1)} %get-tuple-element.146, ...), kind=kOutput, calls=%fused_computation.10.clone.1 | convolution fusion | flops 176685056 | bytes 3014720 | tf_op jit(solution)/shard_map/while/body/lrs,lst->lrt/dot_general | solution.py:66
  384.0 11.2 %fusion.33 = f32[64,16,256]{2,1,0:T(8,128)} fusion(f32[64,16,256]{2,1,0:T(8,128)} %get-tuple-element.159, bf16[64,16,256]{2,1,0:T(8,128)(2,1)S(1)} %gather_fusion, f32[64,256]{1,0:T(8,128)S(1)} %get-tuple-element.142, f32[64,256]{1,0:T(8,128)S(1)} %get-tuple-element.145, f32[64,256]{1,0:T(8,128)S(1)} %get-tuple-element.146, ...), kind=kOutput, calls=%fused_computation.10.clone.1 | convolution fusion | flops 176685056 | bytes 3014720 | tf_op jit(solution)/shard_map/while/body/lrs,lst->lrt/dot_general | solution.py:66
  401.0 11.2 %fusion.33 = f32[64,16,256]{2,1,0:T(8,128)} fusion(f32[64,16,256]{2,1,0:T(8,128)} %get-tuple-element.159, bf16[64,16,256]{2,1,0:T(8,128)(2,1)S(1)} %gather_fusion, f32[64,256]{1,0:T(8,128)S(1)} %get-tuple-element.142, f32[64,256]{1,0:T(8,128)S(1)} %get-tuple-element.145, f32[64,256]{1,0:T(8,128)S(1)} %get-tuple-element.146, ...), kind=kOutput, calls=%fused_computation.10.clone.1 | convolution fusion | flops 176685056 | bytes 3014720 | tf_op jit(solution)/shard_map/while/body/lrs,lst->lrt/dot_general | solution.py:66
  418.1 11.2 %fusion.33 = f32[64,16,256]{2,1,0:T(8,128)} fusion(f32[64,16,256]{2,1,0:T(8,128)} %get-tuple-element.159, bf16[64,16,256]{2,1,0:T(8,128)(2,1)S(1)} %gather_fusion, f32[64,256]{1,0:T(8,128)S(1)} %get-tuple-element.142, f32[64,256]{1,0:T(8,128)S(1)} %get-tuple-element.145, f32[64,256]{1,0:T(8,128)S(1)} %get-tuple-element.146, ...), kind=kOutput, calls=%fused_computation.10.clone.1 | convolution fusion | flops 176685056 | bytes 3014720 | tf_op jit(solution)/shard_map/while/body/lrs,lst->lrt/dot_general | solution.py:66
  435.1 11.2 %fusion.33 = f32[64,16,256]{2,1,0:T(8,128)} fusion(f32[64,16,256]{2,1,0:T(8,128)} %get-tuple-element.159, bf16[64,16,256]{2,1,0:T(8,128)(2,1)S(1)} %gather_fusion, f32[64,256]{1,0:T(8,128)S(1)} %get-tuple-element.142, f32[64,256]{1,0:T(8,128)S(1)} %get-tuple-element.145, f32[64,256]{1,0:T(8,128)S(1)} %get-tuple-element.146, ...), kind=kOutput, calls=%fused_computation.10.clone.1 | convolution fusion | flops 176685056 | bytes 3014720 | tf_op jit(solution)/shard_map/while/body/lrs,lst->lrt/dot_general | solution.py:66
  446.4 3.3 fusion.8
  (183 shorter events, 106.6 us)
Async XLA Ops:
  6.5 19.7 %copy-start = (bf16[64,64,256]{2,1,0:T(8,128)(2,1)S(1)}, bf16[64,64,256]{2,1,0:T(8,128)(2,1)}, u32[]{:S(2)}) copy-start(bf16[64,64,256]{2,1,0:T(8,128)(2,1)} %param.13) | copy-start | bytes 6291460
  6.5 1.1 copy-start.1
  11.3 14.9 %copy-start.2 = (bf16[64,16,256]{2,1,0:T(8,128)(2,1)S(1)}, bf16[64,16,256]{2,1,0:T(8,128)(2,1)}, u32[]{:S(2)}) copy-start(bf16[64,16,256]{2,1,0:T(8,128)(2,1)} %param.12) | copy-start | bytes 1572868
  14.7 28.0 %all-to-all-start.1 = ((bf16[128,4,3,256]{3,1,2,0:T(4,128)(2,1)}), bf16[128,4,3,256]{3,1,2,0:T(4,128)(2,1)S(1)}, u32[]{:S(2)}, u32[]{:S(2)}) async-start(bf16[128,4,3,256]{3,1,2,0:T(4,128)(2,1)} %copy.29), calls=%async_computation.1 | async-start | bytes 1572864 | tf_op jit(solution)/shard_map/all_to_all | solution.py:51
  26.2 129.6 %all-gather.2.cloned.1.call-start = ((), (), s32[]{:S(2)}) async-start(), calls=%async_computation.2 | async-start | bytes 4227072 | tf_op jit(solution)/shard_map/all_gather | solution.py:44
  32.6 16.5 %copy-start.4 = (s32[8,27]{1,0:T(8,128)S(1)}, s32[8,27]{1,0:T(8,128)}, u32[]{:S(2)}) copy-start(s32[8,27]{1,0:T(8,128)} %param.19) | copy-start | bytes 2596
  32.6 16.6 %copy-start.3 = (bf16[8,3,64]{2,0,1:T(8,128)(2,1)S(1)}, bf16[8,3,64]{2,0,1:T(8,128)(2,1)}, u32[]{:S(2)}) copy-start(bf16[8,3,64]{2,0,1:T(8,128)(2,1)} %param.15) | copy-start | bytes 9220
  42.7 125.8 %all-to-all-start = ((bf16[128,4,16,256]{3,2,1,0:T(8,128)(2,1)}), bf16[128,4,16,256]{3,2,1,0:T(8,128)(2,1)}, u32[]{:S(2)}, u32[]{:S(2)}) async-start(bf16[128,4,16,256]{3,2,1,0:T(8,128)(2,1)} %bitcast.78), calls=%async_computation | async-start | bytes 8388608 | tf_op jit(solution)/shard_map/all_to_all | solution.py:52
  168.5 4.8 %copy-start.5 = (s32[64]{0:T(128)S(1)}, s32[64]{0:T(128)}, u32[]{:S(2)}) copy-start(s32[64]{0:T(128)} %param.18) | copy-start | bytes 772
Sparse Core Ops, SparseCore 0:
  30.2 100.4 all-gather.1
where the time goes:
time: 460 us; the launch traced here: 456 us
  matrix products  204 us (44%)
  local copies, waits for them, and re-layouts  113 us (25%)
  blocking collectives  79.3 us (17%)
  other arithmetic  18 us (4%)
  starting transfers between devices  17.3 us (4%)
  between operations  13.5 us (3%)
  waiting for transfers between devices  10.1 us (2%)
    dot_general x16, matrix products, near_step(): jnp.einsum('lrs,lst->lrt', table_charges[slot_index], kernel_vals, prefer...  180 us
    all_gather x1, blocking collectives, body(): lax.all_gather(skeleton, ('grp', 'sub'), axis=0, tiled=True)  79.3 us
    gather x16, local copies, waits for them, and re-layouts, near_step(): table_charges[slot_index]  46.9 us
    gather x16, local copies, waits for them, and re-layouts, near_step(): kernel_vals = kernel_block(coordinates, table_coords[slot_index])  31.4 us
    all_to_all x1, starting transfers between devices, body(): lax.all_to_all(out_coords, ('grp', 'sub'), split_axis=0, concat_axis=0, t...  11.5 us
    select_n x16, other arithmetic, near_step(): table_charges[slot_index]  11.1 us
    dot_general x1, matrix products, body(): jnp.einsum('lrs,lst->lrt', charges, own_kernel, preferred_element_type=jn...  10.3 us
    all_to_all x1, waiting for transfers between devices, body(): lax.all_to_all(out_coords, ('grp', 'sub'), split_axis=0, concat_axis=0, t...  10.1 us
  transfers between devices with their start and end apart: 3, of which 1 were waited for; matrix products, arithmetic and copies ran while one was open for 10% of the time, Pallas kernels for 0%

commit v1 on v0

v1 whole, which is shorter than its diff:
```python
import functools

import jax
import jax.numpy as jnp
from jax import lax
from jax.experimental import pallas as pl
from jax.experimental.pallas import tpu as pltpu
from jax.sharding import PartitionSpec as P

SOFTENING = 0.01
AXES = ("grp", "sub")
BF16 = jnp.bfloat16
F32 = jnp.float32
I32 = jnp.int32
MIB = 1024 * 1024
GROUP = 8
UNROLL = 8

SMEM = pl.BlockSpec(memory_space=pltpu.SMEM)


def whole(shape):
    return pl.BlockSpec(shape, lambda *_: (0,) * len(shape))


def dot_nt(a, b):
    return lax.dot_general(a, b, (((1,), (1,)), ((), ())), preferred_element_type=F32)


def dot_nn(a, b):
    return lax.dot_general(a, b, (((1,), (0,)), ((), ())), preferred_element_type=F32)


def store_rows(table, comps):
    count = comps.shape[1]
    for k in range(8):
        for h in range(2):
            rows = jnp.zeros((count, 128), F32)
            if k % 4 < 3:
                rows = comps[k % 4, :, 128 * h : 128 * h + 128].astype(F32)
            table[h, pl.ds(k, count, stride=8), :] = rows


def pack_kernel(plan, comps, charges, out, table):
    step = pl.program_id(0)
    per_step = out.shape[0]

    @pl.when(step == 0)
    def _():
        store_rows(table, comps)

    first_half = lax.broadcasted_iota(I32, (8, 128), 0) < 4

    def one(e, _):
        rows = [plan[(step * per_step + e) * 4 + c] for c in range(4)]
        for c in range(4):
            out[e, 16 * c : 16 * c + 16, :] = charges[rows[c]]
        halves = []
        for h in range(2):
            pos = [table[h, pl.ds(pl.multiple_of(8 * r, 8), 8), :] for r in rows]
            low = jnp.where(first_half, pos[0], pos[1])
            high = jnp.where(first_half, pos[2], pos[3])
            halves.append(jnp.concatenate([low, high], axis=0))
        out[e, 64:80, :] = jnp.concatenate(halves, axis=1).astype(BF16)
        return 0

    lax.fori_loop(0, per_step, one, 0, unroll=4)


def pack(plan, comps, charges, devices):
    leaves, _, points = charges.shape
    per_step = 16
    return pl.pallas_call(
        pack_kernel,
        grid=(devices // per_step,),
        out_shape=jax.ShapeDtypeStruct((devices, 80, points), BF16),
        in_specs=[SMEM, whole(comps.shape), whole(charges.shape)],
        out_specs=pl.BlockSpec((per_step, 80, points), lambda i: (i, 0, 0)),
        scratch_shapes=[pltpu.VMEM((2, leaves * 8, 128), F32)],
        compiler_params=pltpu.CompilerParams(vmem_limit_bytes=24 * MIB),
        cost_estimate=pl.CostEstimate(flops=0, bytes_accessed=6 * MIB, transcendentals=0),
        name="pack",
    )(plan, comps, charges)


def moments_kernel(charges, basis, transfer, skel, out, table):
    def parent(p):
        total = jnp.zeros((16, 64), F32)
        for i in range(GROUP):
            leaf = p * GROUP + i
            moment = dot_nt(charges[leaf], basis[leaf]).astype(BF16)
            total = total + dot_nn(moment, transfer[leaf])
        return total

    def pair(a, _):
        both = jnp.concatenate([parent(a), parent(a + 4)], axis=1).astype(BF16)
        out[pl.ds(pl.multiple_of(16 * a, 16), 16), :] = both
        return 0

    lax.fori_loop(0, 4, pair, 0)
    table[...] = jnp.zeros_like(table)
    for k in range(3):
        rows = skel[k].astype(F32)
        table[pl.ds(k, 4, stride=4), :] = jnp.concatenate([rows[0:4], rows[4:8]], axis=1)
    out[64:80, :] = table[...].astype(BF16)


def parent_payload(charges, basis, transfer, skel):
    return pl.pallas_call(
        moments_kernel,
        out_shape=jax.ShapeDtypeStruct((80, 128), BF16),
        scratch_shapes=[pltpu.VMEM((16, 128), F32)],
        compiler_params=pltpu.CompilerParams(vmem_limit_bytes=24 * MIB),
        cost_estimate=pl.CostEstimate(flops=10**8, bytes_accessed=4 * MIB, transcendentals=0),
        name="moments",
    )(charges, basis, transfer, skel)


def near_blocks(items, base, steps, targets, row_of, charges_of, acc):
    def body(n, _):
        results = []
        for u in range(UNROLL):
            code = items[base + n * UNROLL + u]
            target = code >> 10
            source = code & 1023
            place = target & 7
            charge = charges_of(source)
            total = None
            for h in range(2):
                lanes = slice(128 * h, 128 * h + 128)
                tiles = []
                wide = []
                for k in range(3):
                    row = jnp.broadcast_to(row_of(h, source, k), (16, 128))
                    wide.append(jnp.concatenate([row, row], axis=1).astype(BF16))
                for q in range(8):
                    square = None
                    for k in range(3):
                        off = targets[place, k, 16 * q : 16 * q + 16, :] - wide[k]
                        square = off * off + BF16(SOFTENING) if k == 0 else square + off * off
                    tiles.append(lax.rsqrt(square))
                values = jnp.concatenate(tiles, axis=0)
                values = jnp.concatenate([values[:, :128], values[:, 128:]], axis=0)
                part = dot_nt(charge[:, lanes], values)
                total = part if total is None else total + part
            results.append((target, total))
        for target, total in results:
            acc[target] += total
        return 0

    lax.fori_loop(0, steps, body, 0)


GHOST_CAP = 8 * 16 + UNROLL


def local_kernel(
    lists, counts, comps, charges, targets, ghost_items, ghost_steps, near, table, acc, items
):
    step = pl.program_id(0)

    @pl.when(step == 0)
    def _():
        store_rows(table, comps)

    def leaf_entries(i, ends):
        local_end, ghost_end = ends
        leaf = step * GROUP + i
        live_count = counts[leaf]
        items[local_end] = i * 1024 + leaf
        local_end = local_end + 1
        for j in range(16):
            slot = lists[j * 64 + leaf]
            live = j < live_count
            is_local = slot < 64
            items[local_end] = i * 1024 + slot
            ghost_items[ghost_end] = i * 1024 + slot - 64
            local_end = local_end + jnp.where(live & is_local, 1, 0)
            ghost_end = ghost_end + jnp.where(live & jnp.logical_not(is_local), 1, 0)
        return local_end, ghost_end

    base = step * GHOST_CAP
    local_end, ghost_end = lax.fori_loop(0, GROUP, leaf_entries, (I32(0), base))
    for u in range(UNROLL):
        items[local_end + u] = 8 * 1024
        ghost_items[ghost_end + u] = 8 * 1024
    ghost_steps[step] = (ghost_end - base + UNROLL - 1) // UNROLL

    def spread(i, _):
        leaf = step * GROUP + i
        cols = [table[h, pl.ds(pl.multiple_of(8 * leaf, 8), 8), :].T for h in range(2)]
        for k in range(3):
            halves = [jnp.broadcast_to(cols[h][:, k : k + 1], (128, 128)) for h in range(2)]
            targets[i, k] = jnp.concatenate(halves, axis=1).astype(BF16)
        return 0

    lax.fori_loop(0, GROUP, spread, 0)

    acc[...] = jnp.zeros_like(acc)
    near_blocks(
        items,
        0,
        (local_end + UNROLL - 1) // UNROLL,
        targets,
        lambda h, s, k: table[h, pl.ds(8 * s + k, 1), :],
        lambda s: charges[s],
        acc,
    )
    near[...] = acc[0:GROUP]


def local_near(lists, counts, comps, charges):
    leaves, rhs, points = charges.shape
    groups = leaves // GROUP
    return pl.pallas_call(
        local_kernel,
        grid=(groups,),
        out_shape=(
            jax.ShapeDtypeStruct((leaves, 3, 128, points), BF16),
            jax.ShapeDtypeStruct((groups * GHOST_CAP,), I32),
            jax.ShapeDtypeStruct((groups,), I32),
            jax.ShapeDtypeStruct((leaves, rhs, points), F32),
        ),
        in_specs=[SMEM, SMEM, whole(comps.shape), whole(charges.shape)],
        out_specs=(
            pl.BlockSpec((GROUP, 3, 128, points), lambda i: (i, 0, 0, 0)),
            SMEM,
            SMEM,
            pl.BlockSpec((GROUP, rhs, points), lambda i: (i, 0, 0)),
        ),
        scratch_shapes=[
            pltpu.VMEM((2, leaves * 8, 128), F32),
            pltpu.VMEM((GROUP + 1, rhs, points), F32),
            pltpu.SMEM((8 * 17 + UNROLL,), I32),
        ],
        compiler_params=pltpu.CompilerParams(vmem_limit_bytes=32 * MIB),
        cost_estimate=pl.CostEstimate(
            flops=2 * 10**9, bytes_accessed=15 * MIB, transcendentals=8 * 10**6
        ),
        name="local_near",
    )(lists, counts, comps, charges)


def ghost_kernel(items, steps, ghosts, targets, start, near, table, acc):
    step = pl.program_id(0)

    @pl.when(step == 0)
    def _():
        def widen(e, _):
            rows = ghosts[e, 64:80, :].astype(F32)
            for h in range(2):
                table[h, pl.ds(pl.multiple_of(16 * e, 16), 16), :] = rows[:, 128 * h : 128 * h + 128]
            return 0

        lax.fori_loop(0, ghosts.shape[0], widen, 0, unroll=8)

    def charges_of(s):
        return ghosts[s >> 2, pl.ds(pl.multiple_of(16 * (s & 3), 16), 16), :]

    acc[0:GROUP] = start[...]
    acc[GROUP] = jnp.zeros(acc.shape[1:], F32)
    near_blocks(
        items,
        step * GHOST_CAP,
        steps[step],
        targets,
        lambda h, s, k: table[h, pl.ds(4 * s + k, 1), :],
        charges_of,
        acc,
    )
    near[...] = acc[0:GROUP]


def ghost_near(items, steps, ghosts, targets, start):
    leaves, rhs, points = start.shape
    devices = ghosts.shape[0]
    block = pl.BlockSpec((GROUP, rhs, points), lambda i: (i, 0, 0))
    return pl.pallas_call(
        ghost_kernel,
        grid=(leaves // GROUP,),
        out_shape=jax.ShapeDtypeStruct(start.shape, F32),
        in_specs=[
            SMEM,
            SMEM,
            whole(ghosts.shape),
            pl.BlockSpec((GROUP, 3, 128, points), lambda i: (i, 0, 0, 0)),
            block,
        ],
        out_specs=block,
        scratch_shapes=[
            pltpu.VMEM((2, devices * 16, 128), F32),
            pltpu.VMEM((GROUP + 1, rhs, points), F32),
        ],
        compiler_params=pltpu.CompilerParams(vmem_limit_bytes=40 * MIB),
        cost_estimate=pl.CostEstimate(
            flops=10**10, bytes_accessed=20 * MIB, transcendentals=4 * 10**7
        ),
        name="ghost_near",
    )(items, steps, ghosts, targets, start)


def finish_kernel(far, parents, skel, transfer, basis, near, out, table, own, *, scales):
    near_scale, far_scale = scales
    step = pl.program_id(0)

    @pl.when(step == 0)
    def _():
        def widen(e, _):
            table[pl.ds(pl.multiple_of(16 * e, 16), 16), :] = parents[e, 64:80, :].astype(F32)
            return 0

        lax.fori_loop(0, parents.shape[0], widen, 0, unroll=8)
        own[...] = jnp.zeros_like(own)
        for k in range(3):
            rows = skel[k].astype(F32)
            own[pl.ds(k, 8, stride=8), :] = jnp.concatenate([rows, rows], axis=1)

    cols = own[pl.ds(pl.multiple_of(8 * step, 8), 8), :].T
    target = [jnp.broadcast_to(cols[0:64, k : k + 1], (64, 128)) for k in range(3)]
    half = (lax.broadcasted_iota(I32, (16, 128), 1) >= 64).astype(I32)

    length = far.shape[0] // 8
    total = jnp.zeros((16, 64), F32)
    for f in range(length):
        parent = far[step * length + f]
        device, place = parent >> 3, parent & 7
        a, b = place & 3, place >> 2
        moment = parents[device, pl.ds(pl.multiple_of(16 * a, 16), 16), :]
        moment = jnp.where(half == b, moment.astype(F32), F32(0.0)).astype(BF16)
        square = None
        for k in range(3):
            off = target[k] - table[pl.ds(device * 16 + 4 * a + k, 1), :]
            square = off * off + SOFTENING if k == 0 else square + off * off
        total = total + dot_nt(moment, lax.rsqrt(square).astype(BF16))
    local = (far_scale * total).astype(BF16)
    for i in range(GROUP):
        child = dot_nt(local, transfer[i]).astype(BF16)
        out[i] = (near_scale * near[i] + dot_nn(child, basis[i])).astype(BF16)


def finish(far, parents, skel, transfer, basis, near, scales):
    leaves, rhs, points = near.shape
    groups = leaves // GROUP
    devices = parents.shape[0]

    def block(shape):
        return pl.BlockSpec((GROUP,) + shape[1:], lambda i: (i, 0, 0))

    return pl.pallas_call(
        functools.partial(finish_kernel, scales=scales),
        grid=(groups,),
        out_shape=jax.ShapeDtypeStruct(near.shape, BF16),
        in_specs=[
            SMEM,
            whole(parents.shape),
            whole(skel.shape),
            block(transfer.shape),
            block(basis.shape),
            block(near.shape),
        ],
        out_specs=block(near.shape),
        scratch_shapes=[pltpu.VMEM((devices * 16, 128), F32), pltpu.VMEM((64, 128), F32)],
        compiler_params=pltpu.CompilerParams(vmem_limit_bytes=24 * MIB),
        cost_estimate=pl.CostEstimate(
            flops=10**8, bytes_accessed=8 * MIB, transcendentals=10**6
        ),
        name="finish",
    )(far, parents, skel, transfer, basis, near)


def body(
    coordinates,
    charges,
    leaf_basis,
    transfer,
    skeleton,
    send_plan,
    near_lists,
    near_count,
    far_lists,
):
    points = charges.shape[2]
    rank = leaf_basis.shape[1]
    devices = send_plan.shape[1]
    scales = (
        float(points * (near_lists.shape[1] + 1)) ** (-0.5),
        float(far_lists.shape[1] * rank) ** (-0.5),
    )
    comps = jnp.transpose(coordinates, (1, 0, 2))
    skel = jnp.transpose(skeleton, (1, 0, 2))
    packed = pack(send_plan.reshape(-1), comps, charges, devices)
    ghosts = lax.all_to_all(packed, AXES, split_axis=0, concat_axis=0, tiled=True)
    payload = parent_payload(charges, leaf_basis, transfer, skel)
    parents = lax.all_gather(payload, AXES, axis=0, tiled=False)
    targets, items, steps, near = local_near(
        near_lists.T.reshape(-1), near_count, comps, charges
    )
    near = ghost_near(items, steps, ghosts, targets, near)
    return finish(far_lists.reshape(-1), parents, skel, transfer, leaf_basis, near, scales)


def solution(mesh):
    split3 = P(AXES, None, None)
    in_specs = (split3,) * 6 + (P(AXES, None), P(AXES), P(AXES, None))
    return jax.shard_map(body, mesh=mesh, in_specs=in_specs, out_specs=split3, check_vma=False)
```

time: 460 us -> 162 us (0.35)
  matrix products: 204 us -> 0 us
  local copies, waits for them, and re-layouts: 113 us -> 18.1 us
  blocking collectives: 79.3 us -> 0 us
  Pallas kernels: 0 us -> 64.3 us
  waiting for transfers between devices: 10.1 us -> 53.6 us
  other arithmetic: 18 us -> 0 us
  starting transfers between devices: 17.3 us -> 11.9 us
    dot_general x20 -> x0, matrix products: 204 us -> none  [the longest x16 180 us: near_step(): jnp.einsum('lrs,lst->lrt', table_charges[slot_index], kernel_vals, prefer...]
    gather x40 -> x0, local copies, waits for them, and re-layouts: 98 us -> none  [the longest x16 46.9 us: near_step(): table_charges[slot_index]]
    all_gather x1 -> x0, blocking collectives: 79.3 us -> none  [body(): lax.all_gather(skeleton, ('grp', 'sub'), axis=0, tiled=True)]
    pallas_call x0 -> x5, Pallas kernels: none -> 64.3 us  [the longest x1 30 us: local_near(): pl.pallas_call(local_kernel, grid=(groups,), out_shape=(jax.ShapeDtypeStr...]
    all_gather x1, waiting for transfers between devices: 0.01 us -> 31.2 us  [body(): parents = lax.all_gather(payload, AXES, axis=0, tiled=False)]
    unnamed x12 -> x37, local copies, waits for them, and re-layouts: 0.03 us -> 17.8 us
    all_to_all x2 -> x1, waiting for transfers between devices: 10.1 us -> 22.4 us  [body(): lax.all_to_all(packed, AXES, split_axis=0, concat_axis=0, tiled=True)]
    select_n x19 -> x0, other arithmetic: 11.9 us -> none  [the longest x16 11.1 us: near_step(): table_charges[slot_index]]
  transfers between devices with their start and end apart: 3 -> 2, of which waited for: 1 -> 2; matrix products, arithmetic and copies ran while one was open for 10% -> 0% of each run, Pallas kernels for 0% -> 29%
where the time goes in v1:
time: 162 us; the launch traced here: 161 us
  Pallas kernels  64.3 us (40%)
  waiting for transfers between devices  53.6 us (33%)
  local copies, waits for them, and re-layouts  18.1 us (11%)
  between operations  13.5 us (8%)
  starting transfers between devices  11.9 us (7%)
    all_gather x1, waiting for transfers between devices, body(): parents = lax.all_gather(payload, AXES, axis=0, tiled=False)  31.2 us
    pallas_call x1, Pallas kernels, local_near(): pl.pallas_call(local_kernel, grid=(groups,), out_shape=(jax.ShapeDtypeStr...  30 us
    all_to_all x1, waiting for transfers between devices, body(): lax.all_to_all(packed, AXES, split_axis=0, concat_axis=0, tiled=True)  22.4 us
    unnamed x37, local copies, waits for them, and re-layouts  17.8 us
    pallas_call x1, Pallas kernels, finish(): pl.pallas_call(functools.partial(finish_kernel, scales=scales), grid=(gro...  15.9 us
    pallas_call x1, Pallas kernels, ghost_near(): pl.pallas_call(ghost_kernel, grid=(leaves // GROUP,), out_shape=jax.Shape...  12.5 us
    all_to_all x1, starting transfers between devices, body(): lax.all_to_all(packed, AXES, split_axis=0, concat_axis=0, tiled=True)  11.9 us
    pallas_call x1, Pallas kernels, parent_payload(): pl.pallas_call(moments_kernel, out_shape=jax.ShapeDtypeStruct((80, 128),...  3.97 us
  transfers between devices with their start and end apart: 2, of which 2 were waited for; matrix products, arithmetic and copies ran while one was open for 0% of the time, Pallas kernels for 29%

profile of v1, /device:TPU:1, one launch (start us, length us, event | category | flops | bytes accessed | tf_op | source)
XLA Modules:
  0.0 161.4 jit_solution(13015285533368614462)
XLA Ops:
  6.5 0.8 copy.10
  7.3 0.1 reshape.11.plan
  7.4 0.0 copy-start.4
  7.4 1.0 copy-done.4
  8.5 0.9 copy-done.9
  9.4 1.9 %pack.1 = bf16[128,80,256]{2,1,0:T(8,128)(2,1)S(1)} custom-call(s32[512]{0:T(512)S(1)} %reshape.11.plan, bf16[3,64,256]{2,1,0:T(8,128)(2,1)S(1)} %bitcast.5, bf16[64,16,256]{2,1,0:T(8,128)(2,1)S(1)} %copy-done.4), custom_call_target="tpu_custom_call" | custom-call | bytes 6291456 | tf_op jit(solution)/shard_map/pack/pallas_call | solution.py:73
  11.3 2.3 %copy-done = bf16[128,80,256]{2,1,0:T(8,128)(2,1)} copy-done((bf16[128,80,256]{2,1,0:T(8,128)(2,1)}, bf16[128,80,256]{2,1,0:T(8,128)(2,1)S(1)}, u32[]{:S(2)}) %copy-start) | copy-done | bytes 5242904
  13.7 0.0 copy-start.16
  13.7 0.0 copy-start.10
  13.7 0.0 copy-start.12
  13.7 11.9 %all-to-all-start = ((bf16[128,80,256]{2,1,0:T(8,128)(2,1)}), bf16[128,80,256]{2,1,0:T(8,128)(2,1)}, u32[]{:S(2)}, u32[]{:S(2)}) async-start(bf16[128,80,256]{2,1,0:T(8,128)(2,1)} %copy-done), calls=%async_computation | async-start | bytes 10485760 | tf_op jit(solution)/shard_map/all_to_all | solution.py:392
  25.6 0.0 all-gather.3.cloned.1.call-start
  25.7 0.0 copy-done.1
  25.7 0.0 copy-done.2
  25.7 0.0 copy-start.5
  25.7 1.0 copy-done.5
  26.7 4.0 %moments.1 = bf16[80,128]{1,0:T(8,128)(2,1)} custom-call(bf16[64,16,256]{2,1,0:T(8,128)(2,1)S(1)} %copy-done.5, bf16[64,64,256]{2,1,0:T(8,128)(2,1)S(1)} %copy-done.1, bf16[64,64,64]{2,1,0:T(8,128)(2,1)S(1)} %copy-done.2, bf16[3,8,64]{2,1,0:T(8,128)(2,1)S(1)} %bitcast.7), custom_call_target="tpu_custom_call" | custom-call | flops 100000000 | bytes 4194304 | tf_op jit(solution)/shard_map/moments/pallas_call | solution.py:109
  30.7 0.0 all-gather.3.cloned.1.call-update
  30.7 0.1 reshape.9.far
  30.8 0.1 reshape.10.lists
  30.9 1.0 copy-done.6
  31.9 30.0 %local_near.1 = (bf16[64,3,128,256]{3,2,1,0:T(8,128)(2,1)S(1)}, s32[1088]{0:T(1024)S(1)}, s32[8]{0:T(128)S(1)}, f32[64,16,256]{2,1,0:T(8,128)S(1)}) custom-call(s32[1024]{0:T(1024)S(1)} %reshape.10.lists, s32[64]{0:T(128)S(1)} %copy-done.12, bf16[3,64,256]{2,1,0:T(8,128)(2,1)S(1)} %bitcast.6, bf16[64,16,256]{2,1,0:T(8,128)(2,1)S(1)} %copy-done.6), custom_call_target="tpu_custom_call" | custom-call | flops 2000000000 | bytes 15728640 | tf_op jit(solution)/shard_map/local_near/pallas_call | solution.py:215
  62.0 4.5 %copy-done.13 = bf16[64,3,128,256]{3,2,1,0:T(8,128)(2,1)} copy-done((bf16[64,3,128,256]{3,2,1,0:T(8,128)(2,1)}, bf16[64,3,128,256]{3,2,1,0:T(8,128)(2,1)S(1)}, u32[]{:S(2)}) %copy-start.13) | copy-done | bytes 12582936
  66.5 1.0 copy-done.14
  67.4 22.4 %all-to-all-done.ghosts = bf16[128,80,256]{2,1,0:T(8,128)(2,1)} async-done(((bf16[128,80,256]{2,1,0:T(8,128)(2,1)}), bf16[128,80,256]{2,1,0:T(8,128)(2,1)}, u32[]{:S(2)}, u32[]{:S(2)}) %all-to-all-start) | async-done | bytes 5242912 | tf_op jit(solution)/shard_map/all_to_all | solution.py:392
  89.8 1.2 copy-done.15
  91.0 12.5 %ghost_near.1.near = f32[64,16,256]{2,1,0:T(8,128)S(1)} custom-call(s32[1088]{0:T(1024)S(1)} %get-tuple-element.9.items, s32[8]{0:T(128)S(1)} %get-tuple-element.10.steps, bf16[128,80,256]{2,1,0:T(8,128)(2,1)} %all-to-all-done.ghosts, bf16[64,3,128,256]{3,2,1,0:T(8,128)(2,1)} %copy-done.13, f32[64,16,256]{2,1,0:T(8,128)S(1)} %copy-done.15), custom_call_target="tpu_custom_call" | custom-call | flops 10000000000 | bytes 20971520 | tf_op jit(solution)/shard_map/ghost_near/pallas_call | solution.py:278
  103.5 1.0 copy-done.7
  104.5 31.2 %all-gather.3.cloned.1.call-done = bf16[10240,128]{1,0:T(8,128)(2,1)} async-done(((bf16[80,128]{1,0:T(8,128)(2,1)}), bf16[10240,128]{1,0:T(8,128)(2,1)}) %all-gather.3.cloned.1.call-update) | async-done | bytes 2621456 | tf_op jit(solution)/shard_map/all_gather | solution.py:394
  135.7 1.7 %copy-done.3 = bf16[10240,128]{1,0:T(8,128)(2,1)S(1)} copy-done((bf16[10240,128]{1,0:T(8,128)(2,1)S(1)}, bf16[10240,128]{1,0:T(8,128)(2,1)}, u32[]{:S(2)}) %copy-start.3) | copy-done | bytes 2621464
  137.4 1.2 copy-done.8
  138.6 15.9 %finish.1 = bf16[64,16,256]{2,1,0:T(8,128)(2,1)} custom-call(s32[216]{0:T(256)S(1)} %reshape.9.far, bf16[128,80,128]{2,1,0:T(8,128)(2,1)S(1)} %bitcast.4, bf16[3,8,64]{2,1,0:T(8,128)(2,1)S(1)} %bitcast.8, bf16[64,64,64]{2,1,0:T(8,128)(2,1)S(1)} %copy-done.2, bf16[64,64,256]{2,1,0:T(8,128)(2,1)S(1)} %copy-done.1, f32[64,16,256]{2,1,0:T(8,128)S(1)} %copy-done.8), custom_call_target="tpu_custom_call" | custom-call | flops 100000000 | bytes 8388608 | tf_op jit(solution)/shard_map/finish/pallas_call | solution.py:349
  (18 shorter events, 0.0 us)
Async XLA Ops:
  7.4 1.0 copy-start.4
  8.5 0.9 copy-start.9
  11.3 2.3 %copy-start = (bf16[128,80,256]{2,1,0:T(8,128)(2,1)}, bf16[128,80,256]{2,1,0:T(8,128)(2,1)S(1)}, u32[]{:S(2)}) copy-start(bf16[128,80,256]{2,1,0:T(8,128)(2,1)S(1)} %pack.1) | copy-start | bytes 15728644
  13.6 12.0 %copy-start.1 = (bf16[64,64,256]{2,1,0:T(8,128)(2,1)S(1)}, bf16[64,64,256]{2,1,0:T(8,128)(2,1)}, u32[]{:S(2)}) copy-start(bf16[64,64,256]{2,1,0:T(8,128)(2,1)} %basis.3) | copy-start | bytes 6291460
  13.6 12.0 %copy-start.2 = (bf16[64,64,64]{2,1,0:T(8,128)(2,1)S(1)}, bf16[64,64,64]{2,1,0:T(8,128)(2,1)}, u32[]{:S(2)}) copy-start(bf16[64,64,64]{2,1,0:T(8,128)(2,1)} %transfer.3) | copy-start | bytes 1572868
  13.6 12.0 %copy-start.11 = (bf16[8,3,64]{2,0,1:T(8,128)(2,1)S(1)}, bf16[8,3,64]{2,0,1:T(8,128)(2,1)}, u32[]{:S(2)}) copy-start(bf16[8,3,64]{2,0,1:T(8,128)(2,1)} %param.13) | copy-start | bytes 9220
  13.6 17.1 %copy-start.17 = (s32[8,27]{1,0:T(8,128)S(1)}, s32[8,27]{1,0:T(8,128)}, u32[]{:S(2)}) copy-start(s32[8,27]{1,0:T(8,128)} %param.17) | copy-start | bytes 2596
  13.7 17.2 %copy-start.16 = (s32[64,16]{0,1:T(8,128)S(1)}, s32[64,16]{0,1:T(8,128)}, u32[]{:S(2)}) copy-start(s32[64,16]{0,1:T(8,128)} %param.15) | copy-start | bytes 12292
  13.7 17.2 %copy-start.10 = (bf16[64,3,256]{2,0,1:T(8,128)(2,1)S(1)}, bf16[64,3,256]{2,0,1:T(8,128)(2,1)}, u32[]{:S(2)}) copy-start(bf16[64,3,256]{2,0,1:T(8,128)(2,1)} %param.9) | copy-start | bytes 294916
  13.7 17.2 %copy-start.12 = (s32[64]{0:T(128)S(1)}, s32[64]{0:T(128)}, u32[]{:S(2)}) copy-start(s32[64]{0:T(128)} %counts.1) | copy-start | bytes 772
  13.7 76.1 %all-to-all-start = ((bf16[128,80,256]{2,1,0:T(8,128)(2,1)}), bf16[128,80,256]{2,1,0:T(8,128)(2,1)}, u32[]{:S(2)}, u32[]{:S(2)}) async-start(bf16[128,80,256]{2,1,0:T(8,128)(2,1)} %copy-done), calls=%async_computation | async-start | bytes 10485760 | tf_op jit(solution)/shard_map/all_to_all | solution.py:392
  25.6 110.1 %all-gather.3.cloned.1.call-start = ((), (), s32[]{:S(2)}) async-start(), calls=%async_computation.1 | async-start | bytes 2641920 | tf_op jit(solution)/shard_map/all_gather | solution.py:394
  25.7 1.0 copy-start.5
  30.9 1.0 copy-start.6
  62.0 4.5 %copy-start.13 = (bf16[64,3,128,256]{3,2,1,0:T(8,128)(2,1)}, bf16[64,3,128,256]{3,2,1,0:T(8,128)(2,1)S(1)}, u32[]{:S(2)}) copy-start(bf16[64,3,128,256]{3,2,1,0:T(8,128)(2,1)S(1)} %get-tuple-element.11.targets) | copy-start | bytes 37748740
  66.5 1.0 copy-start.14
  89.8 1.2 copy-start.15
  103.5 1.0 copy-start.7
  135.7 1.7 %copy-start.3 = (bf16[10240,128]{1,0:T(8,128)(2,1)S(1)}, bf16[10240,128]{1,0:T(8,128)(2,1)}, u32[]{:S(2)}) copy-start(bf16[10240,128]{1,0:T(8,128)(2,1)} %all-gather.3.cloned.1.call-done) | copy-start | bytes 7864324
  137.4 1.2 copy-start.8
Sparse Core Ops, SparseCore 0:
  30.8 104.7 all-gather.2

commit v2 on v1

v2 whole, which is shorter than its diff:
```python
import functools

import jax
import jax.numpy as jnp
from jax import lax
from jax.experimental import pallas as pl
from jax.experimental.pallas import tpu as pltpu
from jax.sharding import PartitionSpec as P

SOFTENING = 0.01
AXES = ("grp", "sub")
BF16 = jnp.bfloat16
F32 = jnp.float32
I32 = jnp.int32
MIB = 1024 * 1024
VMEM_LIMIT = 60 * MIB
GROUP = 8
UNROLL = 16

SMEM = pl.BlockSpec(memory_space=pltpu.SMEM)
VMEM = pl.BlockSpec(memory_space=pltpu.VMEM)
HBM = pl.BlockSpec(memory_space=pltpu.HBM)


def fetch(source, target, semaphore):
    copy = pltpu.make_async_copy(source, target, semaphore)
    copy.start()
    return copy


def whole(shape):
    return pl.BlockSpec(shape, lambda *_: (0,) * len(shape))


def dot_nt(a, b):
    return lax.dot_general(a, b, (((1,), (1,)), ((), ())), preferred_element_type=F32)


def dot_nn(a, b):
    return lax.dot_general(a, b, (((1,), (0,)), ((), ())), preferred_element_type=F32)


def store_rows(table, comps):
    count = comps.shape[1]
    for k in range(8):
        for h in range(2):
            rows = jnp.zeros((count, 128), F32)
            if k % 4 < 3:
                rows = comps[k % 4, :, 128 * h : 128 * h + 128].astype(F32)
            table[h, pl.ds(k, count, stride=8), :] = rows


def pack_kernel(plan, comps_hbm, charges_hbm, out_hbm, comps, charges, table, out, sems):
    first = fetch(comps_hbm, comps, sems.at[0])
    second = fetch(charges_hbm, charges, sems.at[1])
    first.wait()
    store_rows(table, comps)
    second.wait()
    first_half = lax.broadcasted_iota(I32, (8, 128), 0) < 4

    def one(e, _):
        rows = [plan[c, e] for c in range(4)]
        for c in range(4):
            out[e, 16 * c : 16 * c + 16, :] = charges[rows[c]]
        halves = []
        for h in range(2):
            pos = [table[h, pl.ds(pl.multiple_of(8 * r, 8), 8), :] for r in rows]
            low = jnp.where(first_half, pos[0], pos[1])
            high = jnp.where(first_half, pos[2], pos[3])
            halves.append(jnp.concatenate([low, high], axis=0))
        out[e, 64:80, :] = jnp.concatenate(halves, axis=1).astype(BF16)
        return 0

    pieces = sems.shape[0] - 2
    size = out.shape[0] // pieces

    def piece(q):
        span = pl.ds(q * size, size)
        return pltpu.make_async_copy(out.at[span], out_hbm.at[span], sems.at[2 + q])

    for q in range(pieces):
        lax.fori_loop(q * size, (q + 1) * size, one, 0, unroll=4)
        piece(q).start()
    for q in range(pieces):
        piece(q).wait()


def pack(plan, comps, charges):
    leaves, _, points = charges.shape
    devices = plan.shape[1]
    return pl.pallas_call(
        pack_kernel,
        out_shape=jax.ShapeDtypeStruct((devices, 80, points), BF16),
        in_specs=[SMEM, HBM, HBM],
        out_specs=HBM,
        scratch_shapes=[
            pltpu.VMEM(comps.shape, BF16),
            pltpu.VMEM(charges.shape, BF16),
            pltpu.VMEM((2, leaves * 8, 128), F32),
            pltpu.VMEM((devices, 80, points), BF16),
            pltpu.SemaphoreType.DMA((2 + 4,)),
        ],
        compiler_params=pltpu.CompilerParams(vmem_limit_bytes=VMEM_LIMIT),
        cost_estimate=pl.CostEstimate(flops=0, bytes_accessed=6 * MIB, transcendentals=0),
        name="pack",
    )(plan, comps, charges)


def own_blocks():
    row = lax.broadcasted_iota(I32, (64, 256), 0) // 16
    return row == lax.broadcasted_iota(I32, (64, 256), 1) // 64


def moments_kernel(charges, basis, transfer, skel, copies, out, table):
    own = own_blocks()

    def parent(p):
        total = jnp.zeros((16, 64), F32)
        for quad in range(2):
            leaf = p * GROUP + 4 * quad
            sources = charges[pl.ds(leaf, 4)].reshape(64, 256)
            pairs = dot_nt(sources, basis[pl.ds(leaf, 4)].reshape(256, 256))
            pairs = jnp.where(own, pairs, F32(0.0))
            moment = pairs[0:16] + pairs[16:32] + pairs[32:48] + pairs[48:64]
            total = total + dot_nn(
                moment.astype(BF16), transfer[pl.ds(leaf, 4)].reshape(256, 64)
            )
        return total

    for a in range(4):
        both = jnp.concatenate([parent(a), parent(a + 4)], axis=1).astype(BF16)
        out[16 * a : 16 * a + 16, :] = both
    table[...] = jnp.zeros_like(table)
    for k in range(3):
        rows = skel[k].astype(F32)
        table[pl.ds(k, 4, stride=4), :] = jnp.concatenate([rows[0:4], rows[4:8]], axis=1)
    out[64:80, :] = table[...].astype(BF16)

    def copy(e, _):
        copies[e] = out[...]
        return 0

    lax.fori_loop(0, copies.shape[0], copy, 0, unroll=4)


def parent_payload(charges, basis, transfer, skel, devices):
    return pl.pallas_call(
        moments_kernel,
        out_shape=jax.ShapeDtypeStruct((devices, 80, 128), BF16),
        scratch_shapes=[pltpu.VMEM((80, 128), BF16), pltpu.VMEM((16, 128), F32)],
        compiler_params=pltpu.CompilerParams(vmem_limit_bytes=VMEM_LIMIT),
        cost_estimate=pl.CostEstimate(flops=10**8, bytes_accessed=4 * MIB, transcendentals=0),
        name="moments",
    )(charges, basis, transfer, skel)


def near_blocks(items, first, last, targets, row_of, charges_of, acc):
    def some(n, _):
        results = []
        for u in range(UNROLL):
            code = items[n * UNROLL + u]
            target = code >> 10
            source = code & 1023
            place = target & 63
            charge = charges_of(source)
            total = None
            for h in range(2):
                lanes = slice(128 * h, 128 * h + 128)
                tiles = []
                wide = []
                for k in range(3):
                    row = jnp.broadcast_to(row_of(h, source, k), (16, 128))
                    wide.append(jnp.concatenate([row, row], axis=1).astype(BF16))
                for q in range(8):
                    square = None
                    for k in range(3):
                        off = targets[place, k, 16 * q : 16 * q + 16, :] - wide[k]
                        square = off * off + BF16(SOFTENING) if k == 0 else square + off * off
                    tiles.append(lax.rsqrt(square))
                values = jnp.concatenate(tiles, axis=0)
                values = jnp.concatenate([values[:, :128], values[:, 128:]], axis=0)
                part = dot_nt(charge[:, lanes], values)
                total = part if total is None else total + part
            results.append((target, total))
        for target, total in results:
            acc[target] += total
        return 0

    lax.fori_loop(first, last, some, 0)


def local_kernel(
    lists, counts, comps, charges, targets, ghost_items, ghost_start, near, table, acc, items
):
    leaves = charges.shape[0]
    store_rows(table, comps)

    def leaf_entries(leaf, ends):
        local_end, ghost_end = ends
        ghost_start[leaf] = ghost_end
        live_count = counts[leaf]
        items[local_end] = leaf * 1024 + leaf
        local_end = local_end + 1
        for j in range(16):
            slot = lists[j, leaf]
            live = j < live_count
            is_local = slot < 64
            items[local_end] = leaf * 1024 + slot
            ghost_items[ghost_end] = leaf * 1024 + slot - 64
            local_end = local_end + jnp.where(live & is_local, 1, 0)
            ghost_end = ghost_end + jnp.where(live & jnp.logical_not(is_local), 1, 0)
        return local_end, ghost_end

    local_end, ghost_end = lax.fori_loop(0, leaves, leaf_entries, (I32(0), I32(0)))
    for u in range(UNROLL):
        items[local_end + u] = 64 * 1024
        ghost_items[ghost_end + u] = 64 * 1024
    ghost_start[leaves] = ghost_end

    def spread(leaf, _):
        cols = [table[h, pl.ds(pl.multiple_of(8 * leaf, 8), 8), :].T for h in range(2)]
        for k in range(3):
            halves = [jnp.broadcast_to(cols[h][:, k : k + 1], (128, 128)) for h in range(2)]
            targets[leaf, k] = jnp.concatenate(halves, axis=1).astype(BF16)
        return 0

    lax.fori_loop(0, leaves, spread, 0, unroll=2)

    acc[...] = jnp.zeros_like(acc)
    near_blocks(
        items,
        0,
        (local_end + UNROLL - 1) // UNROLL,
        targets,
        lambda h, s, k: table[h, pl.ds(8 * s + k, 1), :],
        lambda s: charges[s],
        acc,
    )
    near[...] = acc[0:leaves]


def local_near(lists, counts, comps, charges):
    leaves, rhs, points = charges.shape
    return pl.pallas_call(
        local_kernel,
        out_shape=(
            jax.ShapeDtypeStruct((leaves, 3, 128, points), BF16),
            jax.ShapeDtypeStruct((leaves * 16 + UNROLL,), I32),
            jax.ShapeDtypeStruct((leaves + 1,), I32),
            jax.ShapeDtypeStruct((leaves, rhs, points), F32),
        ),
        in_specs=[SMEM, SMEM, VMEM, VMEM],
        out_specs=(VMEM, SMEM, SMEM, VMEM),
        scratch_shapes=[
            pltpu.VMEM((2, leaves * 8, 128), F32),
            pltpu.VMEM((leaves + 1, rhs, points), F32),
            pltpu.SMEM((leaves * 17 + UNROLL,), I32),
        ],
        compiler_params=pltpu.CompilerParams(vmem_limit_bytes=VMEM_LIMIT),
        cost_estimate=pl.CostEstimate(
            flops=2 * 10**9, bytes_accessed=15 * MIB, transcendentals=8 * 10**6
        ),
        name="local_near",
    )(lists, counts, comps, charges)


PARTS = 4


def ghost_kernel(
    items, starts, ghosts, targets_hbm, start, near, targets, table, acc, sems
):
    leaves = start.shape[0]
    part = leaves // PARTS

    def piece(q):
        span = pl.ds(q * part, part)
        return pltpu.make_async_copy(targets_hbm.at[span], targets.at[span], sems.at[q])

    for q in range(PARTS):
        piece(q).start()

    def widen(e, _):
        rows = ghosts[e, 64:80, :].astype(F32)
        for h in range(2):
            table[h, pl.ds(pl.multiple_of(16 * e, 16), 16), :] = rows[:, 128 * h : 128 * h + 128]
        return 0

    lax.fori_loop(0, ghosts.shape[0], widen, 0, unroll=8)

    def charges_of(s):
        return ghosts[s >> 2, pl.ds(pl.multiple_of(16 * (s & 3), 16), 16), :]

    acc[0:leaves] = start[...]
    acc[leaves] = jnp.zeros(acc.shape[1:], F32)

    def run(q, _):
        piece(q).wait()
        end = starts[(q + 1) * part]
        last = jnp.where(q == PARTS - 1, (end + UNROLL - 1) // UNROLL, end // UNROLL)
        near_blocks(
            items,
            starts[q * part] // UNROLL,
            last,
            targets,
            lambda h, s, k: table[h, pl.ds(4 * s + k, 1), :],
            charges_of,
            acc,
        )
        return 0

    lax.fori_loop(0, PARTS, run, 0)
    near[...] = acc[0:leaves]


def ghost_near(items, starts, ghosts, targets, start):
    leaves, rhs, points = start.shape
    devices = ghosts.shape[0]
    return pl.pallas_call(
        ghost_kernel,
        out_shape=jax.ShapeDtypeStruct(start.shape, F32),
        in_specs=[SMEM, SMEM, VMEM, HBM, VMEM],
        out_specs=VMEM,
        scratch_shapes=[
            pltpu.VMEM(targets.shape, BF16),
            pltpu.VMEM((2, devices * 16, 128), F32),
            pltpu.VMEM((leaves + 1, rhs, points), F32),
            pltpu.SemaphoreType.DMA((PARTS,)),
        ],
        compiler_params=pltpu.CompilerParams(vmem_limit_bytes=VMEM_LIMIT),
        cost_estimate=pl.CostEstimate(
            flops=10**10, bytes_accessed=20 * MIB, transcendentals=4 * 10**7
        ),
        name="ghost_near",
    )(items, starts, ghosts, targets, start)


def finish_kernel(
    far,
    parents_hbm,
    skel,
    transfer_hbm,
    basis_hbm,
    near_hbm,
    out,
    parents,
    transfer,
    basis,
    near,
    table,
    own,
    local,
    sems,
    *,
    scales,
):
    near_scale, far_scale = scales
    clusters, length = far.shape
    fetches = [
        fetch(source, target, sems.at[n])
        for n, (source, target) in enumerate(
            [
                (parents_hbm, parents),
                (transfer_hbm, transfer),
                (basis_hbm, basis),
                (near_hbm, near),
            ]
        )
    ]
    fetches[0].wait()

    def widen(e, _):
        table[pl.ds(pl.multiple_of(16 * e, 16), 16), :] = parents[e, 64:80, :].astype(F32)
        return 0

    lax.fori_loop(0, parents.shape[0], widen, 0, unroll=8)
    own[...] = jnp.zeros_like(own)
    for k in range(3):
        rows = skel[k].astype(F32)
        own[pl.ds(k, clusters, stride=8), :] = jnp.concatenate([rows, rows], axis=1)

    half = (lax.broadcasted_iota(I32, (16, 128), 1) >= 64).astype(I32)

    def coefficients(p, _):
        cols = own[pl.ds(pl.multiple_of(8 * p, 8), 8), :].T
        target = [
            jnp.broadcast_to(cols[0:64, k : k + 1], (64, 128)).astype(BF16) for k in range(3)
        ]
        target = [jnp.concatenate([t, t], axis=1) for t in target]
        total = jnp.zeros((16, 64), F32)
        for first in range(0, length, 2):
            moments = []
            rows = [[], [], []]
            for f in (first, first + 1):
                parent = far[p, min(f, length - 1)]
                device, place = parent >> 3, parent & 7
                a, b = place & 3, place >> 2
                moment = parents[device, pl.ds(pl.multiple_of(16 * a, 16), 16), :]
                wanted = b if f < length else 2
                moments.append(jnp.where(half == wanted, moment.astype(F32), F32(0.0)))
                for k in range(3):
                    row = table[pl.ds(device * 16 + 4 * a + k, 1), :]
                    rows[k].append(jnp.broadcast_to(row, (16, 128)))
            rows = [jnp.concatenate(r, axis=1).astype(BF16) for r in rows]
            tiles = []
            for q in range(4):
                square = None
                for k in range(3):
                    off = target[k][16 * q : 16 * q + 16, :] - rows[k]
                    square = off * off + BF16(SOFTENING) if k == 0 else square + off * off
                tiles.append(lax.rsqrt(square))
            moment = jnp.concatenate(moments, axis=1).astype(BF16)
            total = total + dot_nt(moment, jnp.concatenate(tiles, axis=0))
        local[p] = (far_scale * total).astype(BF16)
        return 0

    lax.fori_loop(0, clusters, coefficients, 0)

    for copy in fetches[1:]:
        copy.wait()
    block = own_blocks()

    def leaves_of(p, _):
        coef = local[p]
        coef = jnp.concatenate([coef, coef, coef, coef], axis=0)
        for quad in range(2):
            leaf = p * GROUP + 4 * quad
            child = dot_nt(coef, transfer[pl.ds(leaf, 4)].reshape(256, 64))
            child = jnp.where(block, child, F32(0.0)).astype(BF16)
            field = dot_nn(child, basis[pl.ds(leaf, 4)].reshape(256, 256))
            total = near_scale * near[pl.ds(leaf, 4)] + field.reshape(4, 16, 256)
            out[pl.ds(leaf, 4)] = total.astype(BF16)
        return 0

    lax.fori_loop(0, clusters, leaves_of, 0, unroll=4)


def finish(far, parents, skel, transfer, basis, near, scales):
    devices = parents.shape[0]
    return pl.pallas_call(
        functools.partial(finish_kernel, scales=scales),
        out_shape=jax.ShapeDtypeStruct(near.shape, BF16),
        in_specs=[SMEM, HBM, VMEM, HBM, HBM, HBM],
        out_specs=VMEM,
        scratch_shapes=[
            pltpu.VMEM(parents.shape, BF16),
            pltpu.VMEM(transfer.shape, BF16),
            pltpu.VMEM(basis.shape, BF16),
            pltpu.VMEM(near.shape, F32),
            pltpu.VMEM((devices * 16, 128), F32),
            pltpu.VMEM((64, 128), F32),
            pltpu.VMEM((far.shape[0], 16, 64), BF16),
            pltpu.SemaphoreType.DMA((4,)),
        ],
        compiler_params=pltpu.CompilerParams(vmem_limit_bytes=VMEM_LIMIT),
        cost_estimate=pl.CostEstimate(
            flops=10**8, bytes_accessed=8 * MIB, transcendentals=10**6
        ),
        name="finish",
    )(far, parents, skel, transfer, basis, near)


def body(
    coordinates,
    charges,
    leaf_basis,
    transfer,
    skeleton,
    send_plan,
    near_lists,
    near_count,
    far_lists,
):
    points = charges.shape[2]
    rank = leaf_basis.shape[1]
    devices = send_plan.shape[1]
    scales = (
        float(points * (near_lists.shape[1] + 1)) ** (-0.5),
        float(far_lists.shape[1] * rank) ** (-0.5),
    )
    comps = jnp.transpose(coordinates, (1, 0, 2))
    skel = jnp.transpose(skeleton, (1, 0, 2))
    packed = pack(jnp.transpose(send_plan, (0, 2, 1))[0], comps, charges)
    ghosts = lax.all_to_all(packed, AXES, split_axis=0, concat_axis=0, tiled=True)
    payload = parent_payload(charges, leaf_basis, transfer, skel, devices)
    targets, items, starts, near = local_near(near_lists.T, near_count, comps, charges)
    payload, ghosts, near = lax.optimization_barrier((payload, ghosts, near))
    parents = lax.all_to_all(payload, AXES, split_axis=0, concat_axis=0, tiled=True)
    near = ghost_near(items, starts, ghosts, targets, near)
    return finish(far_lists, parents, skel, transfer, leaf_basis, near, scales)


def solution(mesh):
    split3 = P(AXES, None, None)
    in_specs = (split3,) * 6 + (P(AXES, None), P(AXES), P(AXES, None))
    return jax.shard_map(body, mesh=mesh, in_specs=in_specs, out_specs=split3, check_vma=False)
```

time: 162 us -> 135 us (0.83)
  local copies, waits for them, and re-layouts: 18.1 us -> 1.51 us
  between operations: 13.5 us -> 0.04 us
  Pallas kernels: 64.3 us -> 56.6 us
  starting transfers between devices: 11.9 us -> 18.9 us
  waiting for transfers between devices: 53.6 us -> 56 us
    all_gather x1 -> x0, waiting for transfers between devices: 31.2 us -> none  [body(): parents = lax.all_gather(payload, AXES, axis=0, tiled=False)]
    all_to_all x0 -> x1, waiting for transfers between devices: none -> 25.7 us  [body(): lax.all_to_all(payload, AXES, split_axis=0, concat_axis=0, tiled=True)]
    unnamed x37 -> x2, local copies, waits for them, and re-layouts: 17.8 us -> 1.51 us
    all_to_all x1, waiting for transfers between devices: 22.4 us -> 30.2 us  [body(): lax.all_to_all(packed, AXES, split_axis=0, concat_axis=0, tiled=True)]
    pallas_call x5, Pallas kernels: 64.3 us -> 56.6 us  [the longest x1 27.9 us: local_near(): pl.pallas_call(local_kernel, out_shape=(jax.ShapeDtypeStruct((leaves, 3,...]
    all_to_all x0 -> x1, starting transfers between devices: none -> 7.04 us  [body(): lax.all_to_all(payload, AXES, split_axis=0, concat_axis=0, tiled=True)]
  transfers between devices with their start and end apart: 2 -> 2, of which waited for: 2 -> 2; matrix products, arithmetic and copies ran while one was open for 0% -> 0% of each run, Pallas kernels for 29% -> 33%
where the time goes in v2:
time: 135 us; the launch traced here: 133 us
  Pallas kernels  56.6 us (42%)
  waiting for transfers between devices  56 us (41%)
  starting transfers between devices  18.9 us (14%)
  local copies, waits for them, and re-layouts  1.51 us (1%)
    all_to_all x1, waiting for transfers between devices, body(): lax.all_to_all(packed, AXES, split_axis=0, concat_axis=0, tiled=True)  30.2 us
    pallas_call x1, Pallas kernels, local_near(): pl.pallas_call(local_kernel, out_shape=(jax.ShapeDtypeStruct((leaves, 3,...  27.9 us
    all_to_all x1, waiting for transfers between devices, body(): lax.all_to_all(payload, AXES, split_axis=0, concat_axis=0, tiled=True)  25.7 us
    all_to_all x1, starting transfers between devices, body(): lax.all_to_all(packed, AXES, split_axis=0, concat_axis=0, tiled=True)  11.9 us
    pallas_call x1, Pallas kernels, ghost_near(): pl.pallas_call(ghost_kernel, out_shape=jax.ShapeDtypeStruct(start.shape,...  10.4 us
    pallas_call x1, Pallas kernels, finish(): pl.pallas_call(functools.partial(finish_kernel, scales=scales), out_shape...  8.01 us
    all_to_all x1, starting transfers between devices, body(): lax.all_to_all(payload, AXES, split_axis=0, concat_axis=0, tiled=True)  7.04 us
    pallas_call x1, Pallas kernels, parent_payload(): pl.pallas_call(moments_kernel, out_shape=jax.ShapeDtypeStruct((devices, 8...  5.87 us
  transfers between devices with their start and end apart: 2, of which 2 were waited for; matrix products, arithmetic and copies ran while one was open for 0% of the time, Pallas kernels for 33%

profile of v2, /device:TPU:1, one launch (start us, length us, event | category | flops | bytes accessed | tf_op | source)
XLA Modules:
  0.0 133.1 jit_solution(10707302337216544738)
XLA Ops:
  0.0 4.5 %pack.1 = bf16[128,80,256]{2,1,0:T(8,128)(2,1)} custom-call(s32[4,128]{1,0:T(4,128)} %bitcast.10, bf16[3,64,256]{2,1,0:T(8,128)(2,1)} %bitcast.6, bf16[64,16,256]{2,1,0:T(8,128)(2,1)} %charges.3), custom_call_target="tpu_custom_call" | custom-call | bytes 6291456 | tf_op jit(solution)/shard_map/pack/pallas_call | solution.py:91
  4.5 11.9 %all-to-all-start = ((bf16[128,80,256]{2,1,0:T(8,128)(2,1)}), bf16[128,80,256]{2,1,0:T(8,128)(2,1)}, u32[]{:S(2)}, u32[]{:S(2)}) async-start(bf16[128,80,256]{2,1,0:T(8,128)(2,1)} %pack.1), calls=%async_computation | async-start | bytes 10485760 | tf_op jit(solution)/shard_map/all_to_all | solution.py:484
  16.4 5.9 %moments.1 = bf16[128,80,128]{2,1,0:T(8,128)(2,1)} custom-call(bf16[64,16,256]{2,1,0:T(8,128)(2,1)} %charges.3, bf16[64,64,256]{2,1,0:T(8,128)(2,1)} %basis_hbm.1, bf16[64,64,64]{2,1,0:T(8,128)(2,1)} %transfer_hbm.1, bf16[3,8,64]{2,1,0:T(8,128)(2,1)} %bitcast.8), custom_call_target="tpu_custom_call" | custom-call | flops 100000000 | bytes 4194304 | tf_op jit(solution)/shard_map/moments/pallas_call | solution.py:147
  22.3 27.9 %local_near.1 = (bf16[64,3,128,256]{3,2,1,0:T(8,128)(2,1)}, s32[1040]{0:T(1024)}, s32[65]{0:T(128)}, f32[64,16,256]{2,1,0:T(8,128)}) custom-call(s32[16,64]{1,0:T(8,128)} %bitcast.11, s32[64]{0:T(128)} %counts.1, bf16[3,64,256]{2,1,0:T(8,128)(2,1)} %bitcast.7, bf16[64,16,256]{2,1,0:T(8,128)(2,1)} %charges.3), custom_call_target="tpu_custom_call" | custom-call | flops 2000000000 | bytes 15728640 | tf_op jit(solution)/shard_map/local_near/pallas_call | solution.py:244
  50.2 30.2 %all-to-all-done.ghosts = bf16[128,80,256]{2,1,0:T(8,128)(2,1)} async-done(((bf16[128,80,256]{2,1,0:T(8,128)(2,1)}), bf16[128,80,256]{2,1,0:T(8,128)(2,1)}, u32[]{:S(2)}, u32[]{:S(2)}) %all-to-all-start) | async-done | bytes 5242912 | tf_op jit(solution)/shard_map/all_to_all | solution.py:484
  80.4 7.0 %all-to-all-start.1 = ((bf16[128,80,128]{2,1,0:T(8,128)(2,1)}), bf16[128,80,128]{2,1,0:T(8,128)(2,1)S(1)}, u32[]{:S(2)}, u32[]{:S(2)}) async-start(bf16[128,80,128]{2,1,0:T(8,128)(2,1)} %moments.1), calls=%async_computation.1 | async-start | bytes 5242880 | tf_op jit(solution)/shard_map/all_to_all | solution.py:488
  87.5 10.4 %ghost_near.1.near_hbm = f32[64,16,256]{2,1,0:T(8,128)} custom-call(s32[1040]{0:T(1024)} %get-tuple-element.14.items, s32[65]{0:T(128)} %get-tuple-element.15.starts, bf16[128,80,256]{2,1,0:T(8,128)(2,1)} %all-to-all-done.ghosts, bf16[64,3,128,256]{3,2,1,0:T(8,128)(2,1)} %get-tuple-element.17.targets_hbm, f32[64,16,256]{2,1,0:T(8,128)} %get-tuple-element.18.start), custom_call_target="tpu_custom_call" | custom-call | flops 10000000000 | bytes 20971520 | tf_op jit(solution)/shard_map/ghost_near/pallas_call | solution.py:319
  97.9 25.7 %all-to-all-done.1.parents_hbm = bf16[128,80,128]{2,1,0:T(8,128)(2,1)S(1)} async-done(((bf16[128,80,128]{2,1,0:T(8,128)(2,1)}), bf16[128,80,128]{2,1,0:T(8,128)(2,1)S(1)}, u32[]{:S(2)}, u32[]{:S(2)}) %all-to-all-start.1) | async-done | bytes 2621472 | tf_op jit(solution)/shard_map/all_to_all | solution.py:488
  123.6 0.0 copy-start
  123.6 1.5 %copy-done = bf16[128,80,128]{2,1,0:T(8,128)(2,1)} copy-done((bf16[128,80,128]{2,1,0:T(8,128)(2,1)}, bf16[128,80,128]{2,1,0:T(8,128)(2,1)S(1)}, u32[]{:S(2)}) %copy-start) | copy-done | bytes 2621464
  125.1 8.0 %finish.1 = bf16[64,16,256]{2,1,0:T(8,128)(2,1)} custom-call(s32[8,27]{1,0:T(8,128)} %far.1, bf16[128,80,128]{2,1,0:T(8,128)(2,1)} %copy-done, bf16[3,8,64]{2,1,0:T(8,128)(2,1)} %bitcast.9, bf16[64,64,64]{2,1,0:T(8,128)(2,1)} %transfer_hbm.1, bf16[64,64,256]{2,1,0:T(8,128)(2,1)} %basis_hbm.1, f32[64,16,256]{2,1,0:T(8,128)} %ghost_near.1.near_hbm), custom_call_target="tpu_custom_call" | custom-call | flops 100000000 | bytes 8388608 | tf_op jit(solution)/shard_map/finish/pallas_call | solution.py:440
Async XLA Ops:
  4.5 75.9 %all-to-all-start = ((bf16[128,80,256]{2,1,0:T(8,128)(2,1)}), bf16[128,80,256]{2,1,0:T(8,128)(2,1)}, u32[]{:S(2)}, u32[]{:S(2)}) async-start(bf16[128,80,256]{2,1,0:T(8,128)(2,1)} %pack.1), calls=%async_computation | async-start | bytes 10485760 | tf_op jit(solution)/shard_map/all_to_all | solution.py:484
  80.4 43.2 %all-to-all-start.1 = ((bf16[128,80,128]{2,1,0:T(8,128)(2,1)}), bf16[128,80,128]{2,1,0:T(8,128)(2,1)S(1)}, u32[]{:S(2)}, u32[]{:S(2)}) async-start(bf16[128,80,128]{2,1,0:T(8,128)(2,1)} %moments.1), calls=%async_computation.1 | async-start | bytes 5242880 | tf_op jit(solution)/shard_map/all_to_all | solution.py:488
  123.6 1.5 %copy-start = (bf16[128,80,128]{2,1,0:T(8,128)(2,1)}, bf16[128,80,128]{2,1,0:T(8,128)(2,1)S(1)}, u32[]{:S(2)}) copy-start(bf16[128,80,128]{2,1,0:T(8,128)(2,1)S(1)} %all-to-all-done.1.parents_hbm) | copy-start | bytes 7864324

commit v3 on v2

--- a/solution.py
+++ b/solution.py
@@ -13,7 +13,7 @@
 F32 = jnp.float32
 I32 = jnp.int32
 MIB = 1024 * 1024
-VMEM_LIMIT = 60 * MIB
+VMEM_LIMIT = 62 * MIB
 GROUP = 8
 UNROLL = 16
 
@@ -54,21 +54,32 @@
     first = fetch(comps_hbm, comps, sems.at[0])
     second = fetch(charges_hbm, charges, sems.at[1])
     first.wait()
-    store_rows(table, comps)
+    leaves = comps.shape[1]
+    for t in range(3):
+        for n in range(8):
+            k, h = divmod((2 * t + n) % 6, 2)
+            rows = comps[k, :, 128 * h : 128 * h + 128].astype(F32)
+            table[t, pl.ds(n, leaves, stride=8), :] = rows
     second.wait()
-    first_half = lax.broadcasted_iota(I32, (8, 128), 0) < 4
-
-    def one(e, _):
+    place = lax.broadcasted_iota(I32, (8, 128), 0)
+
+    def one(e):
         rows = [plan[c, e] for c in range(4)]
         for c in range(4):
-            out[e, 16 * c : 16 * c + 16, :] = charges[rows[c]]
-        halves = []
-        for h in range(2):
-            pos = [table[h, pl.ds(pl.multiple_of(8 * r, 8), 8), :] for r in rows]
-            low = jnp.where(first_half, pos[0], pos[1])
-            high = jnp.where(first_half, pos[2], pos[3])
-            halves.append(jnp.concatenate([low, high], axis=0))
-        out[e, 64:80, :] = jnp.concatenate(halves, axis=1).astype(BF16)
+            for h in range(2):
+                lanes = slice(128 * h, 128 * h + 128)
+                first_row = 64 * h + 16 * c
+                out[e, first_row : first_row + 16, :] = charges[rows[c], :, lanes]
+        six = []
+        for t, split in ((0, 6), (1, 4), (2, 2)):
+            front = table[t, pl.ds(pl.multiple_of(8 * rows[t], 8), 8), :]
+            back = table[t, pl.ds(pl.multiple_of(8 * rows[t + 1], 8), 8), :]
+            six.append(jnp.where(place < split, front, back))
+        out[e, 128:152, :] = jnp.concatenate(six, axis=0).astype(BF16)
+
+    def four(e):
+        for n in range(4):
+            one(e + n)
         return 0
 
     pieces = sems.shape[0] - 2
@@ -78,27 +89,30 @@
         span = pl.ds(q * size, size)
         return pltpu.make_async_copy(out.at[span], out_hbm.at[span], sems.at[2 + q])
 
-    for q in range(pieces):
-        lax.fori_loop(q * size, (q + 1) * size, one, 0, unroll=4)
+    def some(q, _):
+        lax.fori_loop(0, size // 4, lambda n, _: four(q * size + 4 * n), 0)
         piece(q).start()
+        return 0
+
+    lax.fori_loop(0, pieces, some, 0)
     for q in range(pieces):
         piece(q).wait()
 
 
 def pack(plan, comps, charges):
-    leaves, _, points = charges.shape
+    leaves = charges.shape[0]
     devices = plan.shape[1]
     return pl.pallas_call(
         pack_kernel,
-        out_shape=jax.ShapeDtypeStruct((devices, 80, points), BF16),
+        out_shape=jax.ShapeDtypeStruct((devices, 152, 128), BF16),
         in_specs=[SMEM, HBM, HBM],
         out_specs=HBM,
         scratch_shapes=[
             pltpu.VMEM(comps.shape, BF16),
             pltpu.VMEM(charges.shape, BF16),
-            pltpu.VMEM((2, leaves * 8, 128), F32),
-            pltpu.VMEM((devices, 80, points), BF16),
-            pltpu.SemaphoreType.DMA((2 + 4,)),
+            pltpu.VMEM((3, leaves * 8, 128), F32),
+            pltpu.VMEM((devices, 152, 128), BF16),
+            pltpu.SemaphoreType.DMA((2 + 8,)),
         ],
         compiler_params=pltpu.CompilerParams(vmem_limit_bytes=VMEM_LIMIT),
         cost_estimate=pl.CostEstimate(flops=0, bytes_accessed=6 * MIB, transcendentals=0),
@@ -165,7 +179,6 @@
             charge = charges_of(source)
             total = None
             for h in range(2):
-                lanes = slice(128 * h, 128 * h + 128)
                 tiles = []
                 wide = []
                 for k in range(3):
@@ -179,7 +192,7 @@
                     tiles.append(lax.rsqrt(square))
                 values = jnp.concatenate(tiles, axis=0)
                 values = jnp.concatenate([values[:, :128], values[:, 128:]], axis=0)
-                part = dot_nt(charge[:, lanes], values)
+                part = dot_nt(charge[h], values)
                 total = part if total is None else total + part
             results.append((target, total))
         for target, total in results:
@@ -233,7 +246,7 @@
         (local_end + UNROLL - 1) // UNROLL,
         targets,
         lambda h, s, k: table[h, pl.ds(8 * s + k, 1), :],
-        lambda s: charges[s],
+        lambda s: [charges[s, :, 0:128], charges[s, :, 128:256]],
         acc,
     )
     near[...] = acc[0:leaves]
@@ -268,31 +281,49 @@
 
 
 def ghost_kernel(
-    items, starts, ghosts, targets_hbm, start, near, targets, table, acc, sems
+    items, starts, ghosts_hbm, targets_hbm, start_hbm, near_hbm, ghosts, targets, table, acc, sems
 ):
-    leaves = start.shape[0]
+    leaves = start_hbm.shape[0]
     part = leaves // PARTS
+    senders = ghosts.shape[0] // PARTS
+
+    def arrival(q):
+        span = pl.ds(q * senders, senders)
+        return pltpu.make_async_copy(ghosts_hbm.at[span], ghosts.at[span], sems.at[0, q])
 
     def piece(q):
         span = pl.ds(q * part, part)
-        return pltpu.make_async_copy(targets_hbm.at[span], targets.at[span], sems.at[q])
-
+        return pltpu.make_async_copy(targets_hbm.at[span], targets.at[span], sems.at[1, q])
+
+    def result(q):
+        span = pl.ds(q * part, part)
+        return pltpu.make_async_copy(acc.at[span], near_hbm.at[span], sems.at[2, q])
+
+    for q in range(PARTS):
+        arrival(q).start()
+    begin = fetch(start_hbm, acc.at[pl.ds(0, leaves)], sems.at[3, 0])
     for q in range(PARTS):
         piece(q).start()
+    acc[leaves] = jnp.zeros(acc.shape[1:], F32)
 
     def widen(e, _):
-        rows = ghosts[e, 64:80, :].astype(F32)
-        for h in range(2):
-            table[h, pl.ds(pl.multiple_of(16 * e, 16), 16), :] = rows[:, 128 * h : 128 * h + 128]
-        return 0
-
-    lax.fori_loop(0, ghosts.shape[0], widen, 0, unroll=8)
+        rows = ghosts[e, 128:152, :].astype(F32)
+        table[pl.ds(pl.multiple_of(24 * e, 8), 24), :] = rows
+        return 0
+
+    def arrived(q, _):
+        arrival(q).wait()
+        lax.fori_loop(0, senders, lambda n, _: widen(q * senders + n, _), 0, unroll=8)
+        return 0
+
+    lax.fori_loop(0, PARTS, arrived, 0)
+    begin.wait()
 
     def charges_of(s):
-        return ghosts[s >> 2, pl.ds(pl.multiple_of(16 * (s & 3), 16), 16), :]
-
-    acc[0:leaves] = start[...]
-    acc[leaves] = jnp.zeros(acc.shape[1:], F32)
+        return [
+            ghosts[s >> 2, pl.ds(pl.multiple_of(64 * h + 16 * (s & 3), 16), 16), :]
+            for h in range(2)
+        ]
 
     def run(q, _):
         piece(q).wait()
@@ -303,14 +334,21 @@
             starts[q * part] // UNROLL,
             last,
             targets,
-            lambda h, s, k: table[h, pl.ds(4 * s + k, 1), :],
+            lambda h, s, k: table[pl.ds(6 * s + 2 * k + h, 1), :],
             charges_of,
             acc,
         )
+
+        @pl.when(q > 0)
+        def _():
+            result(q - 1).start()
+
         return 0
 
     lax.fori_loop(0, PARTS, run, 0)
-    near[...] = acc[0:leaves]
+    result(PARTS - 1).start()
+    for q in range(PARTS):
+        result(q).wait()
 
 
 def ghost_near(items, starts, ghosts, targets, start):
@@ -319,13 +357,14 @@
     return pl.pallas_call(
         ghost_kernel,
         out_shape=jax.ShapeDtypeStruct(start.shape, F32),
-        in_specs=[SMEM, SMEM, VMEM, HBM, VMEM],
-        out_specs=VMEM,
+        in_specs=[SMEM, SMEM, HBM, HBM, HBM],
+        out_specs=HBM,
         scratch_shapes=[
+            pltpu.VMEM(ghosts.shape, BF16),
             pltpu.VMEM(targets.shape, BF16),
-            pltpu.VMEM((2, devices * 16, 128), F32),
+            pltpu.VMEM((devices * 24, 128), F32),
             pltpu.VMEM((leaves + 1, rhs, points), F32),
-            pltpu.SemaphoreType.DMA((PARTS,)),
+            pltpu.SemaphoreType.DMA((4, PARTS)),
         ],
         compiler_params=pltpu.CompilerParams(vmem_limit_bytes=VMEM_LIMIT),
         cost_estimate=pl.CostEstimate(
@@ -337,13 +376,12 @@
 
 def finish_kernel(
     far,
-    parents_hbm,
+    parents,
     skel,
     transfer_hbm,
     basis_hbm,
     near_hbm,
     out,
-    parents,
     transfer,
     basis,
     near,
@@ -360,14 +398,12 @@
         fetch(source, target, sems.at[n])
         for n, (source, target) in enumerate(
             [
-                (parents_hbm, parents),
                 (transfer_hbm, transfer),
                 (basis_hbm, basis),
                 (near_hbm, near),
             ]
         )
     ]
-    fetches[0].wait()
 
     def widen(e, _):
         table[pl.ds(pl.multiple_of(16 * e, 16), 16), :] = parents[e, 64:80, :].astype(F32)
@@ -414,9 +450,9 @@
         local[p] = (far_scale * total).astype(BF16)
         return 0
 
-    lax.fori_loop(0, clusters, coefficients, 0)
-
-    for copy in fetches[1:]:
+    lax.fori_loop(0, clusters, coefficients, 0, unroll=2)
+
+    for copy in fetches:
         copy.wait()
     block = own_blocks()
 
@@ -440,17 +476,16 @@
     return pl.pallas_call(
         functools.partial(finish_kernel, scales=scales),
         out_shape=jax.ShapeDtypeStruct(near.shape, BF16),
-        in_specs=[SMEM, HBM, VMEM, HBM, HBM, HBM],
+        in_specs=[SMEM, VMEM, VMEM, HBM, HBM, HBM],
         out_specs=VMEM,
         scratch_shapes=[
-            pltpu.VMEM(parents.shape, BF16),
             pltpu.VMEM(transfer.shape, BF16),
             pltpu.VMEM(basis.shape, BF16),
             pltpu.VMEM(near.shape, F32),
             pltpu.VMEM((devices * 16, 128), F32),
             pltpu.VMEM((64, 128), F32),
             pltpu.VMEM((far.shape[0], 16, 64), BF16),
-            pltpu.SemaphoreType.DMA((4,)),
+            pltpu.SemaphoreType.DMA((3,)),
         ],
         compiler_params=pltpu.CompilerParams(vmem_limit_bytes=VMEM_LIMIT),
         cost_estimate=pl.CostEstimate(

time: 135 us -> 127 us (0.941); the launches traced: 133 us -> 127 us
  waiting for transfers between devices: 56 us -> 46 us
  Pallas kernels: 56.6 us -> 61.7 us
  local copies, waits for them, and re-layouts: 1.51 us -> 0 us
    all_to_all x1, waiting for transfers between devices: 25.7 us -> 19.5 us  [body(): lax.all_to_all(payload, AXES, split_axis=0, concat_axis=0, tiled=True)]
    pallas_call x1, Pallas kernels: 10.4 us -> 16.4 us  [ghost_near(): pl.pallas_call(ghost_kernel, out_shape=jax.ShapeDtypeStruct(start.shape,...]
    all_to_all x1, waiting for transfers between devices: 30.2 us -> 26.6 us  [body(): lax.all_to_all(packed, AXES, split_axis=0, concat_axis=0, tiled=True)]
    pallas_call x1, Pallas kernels: 8.01 us -> 6.27 us  [finish(): pl.pallas_call(functools.partial(finish_kernel, scales=scales), out_shape...]
    unnamed x2 -> x0, local copies, waits for them, and re-layouts: 1.51 us -> none
  transfers between devices with their start and end apart: 2 -> 2, of which waited for: 2 -> 2; matrix products, arithmetic and copies ran while one was open for 0% -> 0% of each run, Pallas kernels for 33% -> 40%
where the time goes in v3:
time: 127 us
  Pallas kernels  61.7 us (49%)
  waiting for transfers between devices  46 us (36%)
  starting transfers between devices  19 us (15%)
    pallas_call x1, Pallas kernels, local_near(): pl.pallas_call(local_kernel, out_shape=(jax.ShapeDtypeStruct((leaves, 3,...  28.8 us
    all_to_all x1, waiting for transfers between devices, body(): lax.all_to_all(packed, AXES, split_axis=0, concat_axis=0, tiled=True)  26.6 us
    all_to_all x1, waiting for transfers between devices, body(): lax.all_to_all(payload, AXES, split_axis=0, concat_axis=0, tiled=True)  19.5 us
    pallas_call x1, Pallas kernels, ghost_near(): pl.pallas_call(ghost_kernel, out_shape=jax.ShapeDtypeStruct(start.shape,...  16.4 us
    all_to_all x1, starting transfers between devices, body(): lax.all_to_all(packed, AXES, split_axis=0, concat_axis=0, tiled=True)  11.9 us
    all_to_all x1, starting transfers between devices, body(): lax.all_to_all(payload, AXES, split_axis=0, concat_axis=0, tiled=True)  7.08 us
    pallas_call x1, Pallas kernels, finish(): pl.pallas_call(functools.partial(finish_kernel, scales=scales), out_shape...  6.27 us
    pallas_call x1, Pallas kernels, parent_payload(): pl.pallas_call(moments_kernel, out_shape=jax.ShapeDtypeStruct((devices, 8...  5.81 us
  transfers between devices with their start and end apart: 2, of which 2 were waited for; matrix products, arithmetic and copies ran while one was open for 0% of the time, Pallas kernels for 40%

profile of v3, /device:TPU:1, one launch (start us, length us, event | category | flops | bytes accessed | tf_op | source)
XLA Modules:
  0.0 126.8 jit_solution(673935775449584292)
XLA Ops:
  0.0 4.5 %pack.1 = bf16[128,152,128]{2,1,0:T(8,128)(2,1)} custom-call(s32[4,128]{1,0:T(4,128)} %bitcast.10, bf16[3,64,256]{2,1,0:T(8,128)(2,1)} %bitcast.6, bf16[64,16,256]{2,1,0:T(8,128)(2,1)} %charges.3), custom_call_target="tpu_custom_call" | custom-call | bytes 6291456 | tf_op jit(solution)/shard_map/pack/pallas_call | solution.py:105
  4.5 11.9 %all-to-all-start = ((bf16[128,152,128]{2,1,0:T(8,128)(2,1)}), bf16[128,152,128]{2,1,0:T(8,128)(2,1)}, u32[]{:S(2)}, u32[]{:S(2)}) async-start(bf16[128,152,128]{2,1,0:T(8,128)(2,1)} %pack.1), calls=%async_computation | async-start | bytes 9961472 | tf_op jit(solution)/shard_map/all_to_all | solution.py:519
  16.4 5.8 %moments.1 = bf16[128,80,128]{2,1,0:T(8,128)(2,1)} custom-call(bf16[64,16,256]{2,1,0:T(8,128)(2,1)} %charges.3, bf16[64,64,256]{2,1,0:T(8,128)(2,1)} %basis_hbm.1, bf16[64,64,64]{2,1,0:T(8,128)(2,1)} %transfer_hbm.1, bf16[3,8,64]{2,1,0:T(8,128)(2,1)} %bitcast.8), custom_call_target="tpu_custom_call" | custom-call | flops 100000000 | bytes 4194304 | tf_op jit(solution)/shard_map/moments/pallas_call | solution.py:161
  22.2 28.8 %local_near.1 = (bf16[64,3,128,256]{3,2,1,0:T(8,128)(2,1)}, s32[1040]{0:T(1024)}, s32[65]{0:T(128)}, f32[64,16,256]{2,1,0:T(8,128)}) custom-call(s32[16,64]{1,0:T(8,128)} %bitcast.11, s32[64]{0:T(128)} %counts.1, bf16[3,64,256]{2,1,0:T(8,128)(2,1)} %bitcast.7, bf16[64,16,256]{2,1,0:T(8,128)(2,1)} %charges.3), custom_call_target="tpu_custom_call" | custom-call | flops 2000000000 | bytes 15728640 | tf_op jit(solution)/shard_map/local_near/pallas_call | solution.py:257
  51.0 26.6 %all-to-all-done.ghosts_hbm = bf16[128,152,128]{2,1,0:T(8,128)(2,1)} async-done(((bf16[128,152,128]{2,1,0:T(8,128)(2,1)}), bf16[128,152,128]{2,1,0:T(8,128)(2,1)}, u32[]{:S(2)}, u32[]{:S(2)}) %all-to-all-start) | async-done | bytes 4980768 | tf_op jit(solution)/shard_map/all_to_all | solution.py:519
  77.6 7.1 %all-to-all-start.1 = ((bf16[128,80,128]{2,1,0:T(8,128)(2,1)}), bf16[128,80,128]{2,1,0:T(8,128)(2,1)}, u32[]{:S(2)}, u32[]{:S(2)}) async-start(bf16[128,80,128]{2,1,0:T(8,128)(2,1)} %moments.1), calls=%async_computation.1 | async-start | bytes 5242880 | tf_op jit(solution)/shard_map/all_to_all | solution.py:523
  84.6 16.4 %ghost_near.1.near_hbm = f32[64,16,256]{2,1,0:T(8,128)} custom-call(s32[1040]{0:T(1024)} %get-tuple-element.14.items, s32[65]{0:T(128)} %get-tuple-element.15.starts, bf16[128,152,128]{2,1,0:T(8,128)(2,1)} %all-to-all-done.ghosts_hbm, bf16[64,3,128,256]{3,2,1,0:T(8,128)(2,1)} %get-tuple-element.17.targets_hbm, f32[64,16,256]{2,1,0:T(8,128)} %get-tuple-element.18.start_hbm), custom_call_target="tpu_custom_call" | custom-call | flops 10000000000 | bytes 20971520 | tf_op jit(solution)/shard_map/ghost_near/pallas_call | solution.py:357
  101.0 19.5 %all-to-all-done.1.parents = bf16[128,80,128]{2,1,0:T(8,128)(2,1)} async-done(((bf16[128,80,128]{2,1,0:T(8,128)(2,1)}), bf16[128,80,128]{2,1,0:T(8,128)(2,1)}, u32[]{:S(2)}, u32[]{:S(2)}) %all-to-all-start.1) | async-done | bytes 2621472 | tf_op jit(solution)/shard_map/all_to_all | solution.py:523
  120.5 6.3 %finish.1 = bf16[64,16,256]{2,1,0:T(8,128)(2,1)} custom-call(s32[8,27]{1,0:T(8,128)} %far.1, bf16[128,80,128]{2,1,0:T(8,128)(2,1)} %all-to-all-done.1.parents, bf16[3,8,64]{2,1,0:T(8,128)(2,1)} %bitcast.9, bf16[64,64,64]{2,1,0:T(8,128)(2,1)} %transfer_hbm.1, bf16[64,64,256]{2,1,0:T(8,128)(2,1)} %basis_hbm.1, f32[64,16,256]{2,1,0:T(8,128)} %ghost_near.1.near_hbm), custom_call_target="tpu_custom_call" | custom-call | flops 100000000 | bytes 8388608 | tf_op jit(solution)/shard_map/finish/pallas_call | solution.py:476
Async XLA Ops:
  4.5 73.1 %all-to-all-start = ((bf16[128,152,128]{2,1,0:T(8,128)(2,1)}), bf16[128,152,128]{2,1,0:T(8,128)(2,1)}, u32[]{:S(2)}, u32[]{:S(2)}) async-start(bf16[128,152,128]{2,1,0:T(8,128)(2,1)} %pack.1), calls=%async_computation | async-start | bytes 9961472 | tf_op jit(solution)/shard_map/all_to_all | solution.py:519
  77.6 42.9 %all-to-all-start.1 = ((bf16[128,80,128]{2,1,0:T(8,128)(2,1)}), bf16[128,80,128]{2,1,0:T(8,128)(2,1)}, u32[]{:S(2)}, u32[]{:S(2)}) async-start(bf16[128,80,128]{2,1,0:T(8,128)(2,1)} %moments.1), calls=%async_computation.1 | async-start | bytes 5242880 | tf_op jit(solution)/shard_map/all_to_all | solution.py:523

commit v4 on v3

--- a/solution.py
+++ b/solution.py
@@ -5,10 +5,12 @@
 from jax import lax
 from jax.experimental import pallas as pl
 from jax.experimental.pallas import tpu as pltpu
+from jax.sharding import Mesh
 from jax.sharding import PartitionSpec as P
 
 SOFTENING = 0.01
-AXES = ("grp", "sub")
+AXES = ("x", "y", "z", "core")
+RING = 4
 BF16 = jnp.bfloat16
 F32 = jnp.float32
 I32 = jnp.int32
@@ -50,9 +52,12 @@
             table[h, pl.ds(k, count, stride=8), :] = rows
 
 
-def pack_kernel(plan, comps_hbm, charges_hbm, out_hbm, comps, charges, table, out, sems):
+def pack_kernel(
+    plan_hbm, comps_hbm, charges_hbm, out_hbm, comps, charges, table, out, plan, sems
+):
     first = fetch(comps_hbm, comps, sems.at[0])
     second = fetch(charges_hbm, charges, sems.at[1])
+    third = fetch(plan_hbm, plan, sems.at[2])
     first.wait()
     leaves = comps.shape[1]
     for t in range(3):
@@ -61,6 +66,7 @@
             rows = comps[k, :, 128 * h : 128 * h + 128].astype(F32)
             table[t, pl.ds(n, leaves, stride=8), :] = rows
     second.wait()
+    third.wait()
     place = lax.broadcasted_iota(I32, (8, 128), 0)
 
     def one(e):
@@ -82,12 +88,12 @@
             one(e + n)
         return 0
 
-    pieces = sems.shape[0] - 2
+    pieces = sems.shape[0] - 3
     size = out.shape[0] // pieces
 
     def piece(q):
         span = pl.ds(q * size, size)
-        return pltpu.make_async_copy(out.at[span], out_hbm.at[span], sems.at[2 + q])
+        return pltpu.make_async_copy(out.at[span], out_hbm.at[span], sems.at[3 + q])
 
     def some(q, _):
         lax.fori_loop(0, size // 4, lambda n, _: four(q * size + 4 * n), 0)
@@ -105,14 +111,15 @@
     return pl.pallas_call(
         pack_kernel,
         out_shape=jax.ShapeDtypeStruct((devices, 152, 128), BF16),
-        in_specs=[SMEM, HBM, HBM],
+        in_specs=[HBM, HBM, HBM],
         out_specs=HBM,
         scratch_shapes=[
             pltpu.VMEM(comps.shape, BF16),
             pltpu.VMEM(charges.shape, BF16),
             pltpu.VMEM((3, leaves * 8, 128), F32),
             pltpu.VMEM((devices, 152, 128), BF16),
-            pltpu.SemaphoreType.DMA((2 + 8,)),
+            pltpu.SMEM(plan.shape, I32),
+            pltpu.SemaphoreType.DMA((3 + 8,)),
         ],
         compiler_params=pltpu.CompilerParams(vmem_limit_bytes=VMEM_LIMIT),
         cost_estimate=pl.CostEstimate(flops=0, bytes_accessed=6 * MIB, transcendentals=0),
@@ -125,7 +132,7 @@
     return row == lax.broadcasted_iota(I32, (64, 256), 1) // 64
 
 
-def moments_kernel(charges, basis, transfer, skel, copies, out, table):
+def moments_kernel(charges, basis, transfer, skel, out, table):
     own = own_blocks()
 
     def parent(p):
@@ -147,25 +154,51 @@
     table[...] = jnp.zeros_like(table)
     for k in range(3):
         rows = skel[k].astype(F32)
-        table[pl.ds(k, 4, stride=4), :] = jnp.concatenate([rows[0:4], rows[4:8]], axis=1)
+        table[pl.ds(k, 4, stride=3), :] = jnp.concatenate([rows[0:4], rows[4:8]], axis=1)
     out[64:80, :] = table[...].astype(BF16)
 
-    def copy(e, _):
-        copies[e] = out[...]
-        return 0
-
-    lax.fori_loop(0, copies.shape[0], copy, 0, unroll=4)
-
-
-def parent_payload(charges, basis, transfer, skel, devices):
+
+def parent_payload(charges, basis, transfer, skel):
     return pl.pallas_call(
         moments_kernel,
-        out_shape=jax.ShapeDtypeStruct((devices, 80, 128), BF16),
-        scratch_shapes=[pltpu.VMEM((80, 128), BF16), pltpu.VMEM((16, 128), F32)],
+        out_shape=jax.ShapeDtypeStruct((80, 128), BF16),
+        scratch_shapes=[pltpu.VMEM((16, 128), F32)],
         compiler_params=pltpu.CompilerParams(vmem_limit_bytes=VMEM_LIMIT),
         cost_estimate=pl.CostEstimate(flops=10**8, bytes_accessed=4 * MIB, transcendentals=0),
         name="moments",
     )(charges, basis, transfer, skel)
+
+
+def ring_kernel(*refs):
+    pieces, (out, rows, held, sems) = refs[:-4], refs[-4:]
+    for t, piece in enumerate(pieces):
+        held[64 * t : 64 * t + 64, :] = piece[0:64, :]
+        rows[12 * t : 12 * t + 16, :] = piece[64:80, :].astype(F32)
+    held[256:304, :] = rows[0:48, :].astype(BF16)
+    leaving = [fetch(held, out.at[g], sems.at[g]) for g in range(out.shape[0])]
+    for copy in leaving:
+        copy.wait()
+
+
+def ring_copies(payload, groups):
+    pieces = [payload]
+    for dx in range(1, RING):
+        pieces.append(lax.ppermute(payload, "x", [(x, (x + dx) % RING) for x in range(RING)]))
+    lanes = payload.shape[1]
+    return pl.pallas_call(
+        ring_kernel,
+        out_shape=jax.ShapeDtypeStruct((groups, 304, lanes), BF16),
+        in_specs=[VMEM] * RING,
+        out_specs=HBM,
+        scratch_shapes=[
+            pltpu.VMEM((64, lanes), F32),
+            pltpu.VMEM((304, lanes), BF16),
+            pltpu.SemaphoreType.DMA((groups,)),
+        ],
+        compiler_params=pltpu.CompilerParams(vmem_limit_bytes=VMEM_LIMIT),
+        cost_estimate=pl.CostEstimate(flops=0, bytes_accessed=3 * MIB, transcendentals=0),
+        name="ring_copies",
+    )(*pieces)
 
 
 def near_blocks(items, first, last, targets, row_of, charges_of, acc):
@@ -302,8 +335,7 @@
     for q in range(PARTS):
         arrival(q).start()
     begin = fetch(start_hbm, acc.at[pl.ds(0, leaves)], sems.at[3, 0])
-    for q in range(PARTS):
-        piece(q).start()
+    piece(0).start()
     acc[leaves] = jnp.zeros(acc.shape[1:], F32)
 
     def widen(e, _):
@@ -318,6 +350,8 @@
 
     lax.fori_loop(0, PARTS, arrived, 0)
     begin.wait()
+    for q in range(1, PARTS):
+        piece(q).start()
 
     def charges_of(s):
         return [
@@ -338,15 +372,11 @@
             charges_of,
             acc,
         )
-
-        @pl.when(q > 0)
-        def _():
-            result(q - 1).start()
-
         return 0
 
     lax.fori_loop(0, PARTS, run, 0)
-    result(PARTS - 1).start()
+    for q in range(PARTS):
+        result(q).start()
     for q in range(PARTS):
         result(q).wait()
 
@@ -381,6 +411,7 @@
     transfer_hbm,
     basis_hbm,
     near_hbm,
+    out_hbm,
     out,
     transfer,
     basis,
@@ -406,10 +437,10 @@
     ]
 
     def widen(e, _):
-        table[pl.ds(pl.multiple_of(16 * e, 16), 16), :] = parents[e, 64:80, :].astype(F32)
-        return 0
-
-    lax.fori_loop(0, parents.shape[0], widen, 0, unroll=8)
+        table[pl.ds(pl.multiple_of(48 * e, 16), 48), :] = parents[e, 256:304, :].astype(F32)
+        return 0
+
+    lax.fori_loop(0, parents.shape[0], widen, 0, unroll=4)
     own[...] = jnp.zeros_like(own)
     for k in range(3):
         rows = skel[k].astype(F32)
@@ -428,14 +459,13 @@
             moments = []
             rows = [[], [], []]
             for f in (first, first + 1):
-                parent = far[p, min(f, length - 1)]
-                device, place = parent >> 3, parent & 7
-                a, b = place & 3, place >> 2
-                moment = parents[device, pl.ds(pl.multiple_of(16 * a, 16), 16), :]
-                wanted = b if f < length else 2
+                code = far[p, min(f, length - 1)]
+                group, inner, wanted = code >> 8, code & 15, (code >> 4) & 1
+                wanted = wanted if f < length else 2
+                moment = parents[group, pl.ds(pl.multiple_of(16 * inner, 16), 16), :]
                 moments.append(jnp.where(half == wanted, moment.astype(F32), F32(0.0)))
                 for k in range(3):
-                    row = table[pl.ds(device * 16 + 4 * a + k, 1), :]
+                    row = table[pl.ds(48 * group + 3 * inner + k, 1), :]
                     rows[k].append(jnp.broadcast_to(row, (16, 128)))
             rows = [jnp.concatenate(r, axis=1).astype(BF16) for r in rows]
             tiles = []
@@ -456,7 +486,7 @@
         copy.wait()
     block = own_blocks()
 
-    def leaves_of(p, _):
+    def leaves_of(p):
         coef = local[p]
         coef = jnp.concatenate([coef, coef, coef, coef], axis=0)
         for quad in range(2):
@@ -466,26 +496,38 @@
             field = dot_nn(child, basis[pl.ds(leaf, 4)].reshape(256, 256))
             total = near_scale * near[pl.ds(leaf, 4)] + field.reshape(4, 16, 256)
             out[pl.ds(leaf, 4)] = total.astype(BF16)
-        return 0
-
-    lax.fori_loop(0, clusters, leaves_of, 0, unroll=4)
+
+    def half_of(n):
+        span = pl.ds(n * 4 * GROUP, 4 * GROUP)
+        return pltpu.make_async_copy(out.at[span], out_hbm.at[span], sems.at[3 + n])
+
+    def half_leaves(n, _):
+        for p in range(4):
+            leaves_of(4 * n + p)
+        half_of(n).start()
+        return 0
+
+    lax.fori_loop(0, 2, half_leaves, 0)
+    for n in range(2):
+        half_of(n).wait()
 
 
 def finish(far, parents, skel, transfer, basis, near, scales):
-    devices = parents.shape[0]
+    devices = parents.shape[0] * RING
     return pl.pallas_call(
         functools.partial(finish_kernel, scales=scales),
         out_shape=jax.ShapeDtypeStruct(near.shape, BF16),
         in_specs=[SMEM, VMEM, VMEM, HBM, HBM, HBM],
-        out_specs=VMEM,
+        out_specs=HBM,
         scratch_shapes=[
+            pltpu.VMEM(near.shape, BF16),
             pltpu.VMEM(transfer.shape, BF16),
             pltpu.VMEM(basis.shape, BF16),
             pltpu.VMEM(near.shape, F32),
-            pltpu.VMEM((devices * 16, 128), F32),
+            pltpu.VMEM((devices * 12, 128), F32),
             pltpu.VMEM((64, 128), F32),
             pltpu.VMEM((far.shape[0], 16, 64), BF16),
-            pltpu.SemaphoreType.DMA((3,)),
+            pltpu.SemaphoreType.DMA((3 + 2,)),
         ],
         compiler_params=pltpu.CompilerParams(vmem_limit_bytes=VMEM_LIMIT),
         cost_estimate=pl.CostEstimate(
@@ -517,15 +559,21 @@
     skel = jnp.transpose(skeleton, (1, 0, 2))
     packed = pack(jnp.transpose(send_plan, (0, 2, 1))[0], comps, charges)
     ghosts = lax.all_to_all(packed, AXES, split_axis=0, concat_axis=0, tiled=True)
-    payload = parent_payload(charges, leaf_basis, transfer, skel, devices)
+    payload = parent_payload(charges, leaf_basis, transfer, skel)
+    payload = ring_copies(payload, devices // RING)
     targets, items, starts, near = local_near(near_lists.T, near_count, comps, charges)
-    payload, ghosts, near = lax.optimization_barrier((payload, ghosts, near))
-    parents = lax.all_to_all(payload, AXES, split_axis=0, concat_axis=0, tiled=True)
+    apart = (lax.axis_index("x") - (far_lists >> 8)) & 3
+    codes = ((far_lists >> 3) & 31) << 8 | (far_lists >> 2 & 1) << 4 | apart << 2 | far_lists & 3
+    payload, ghosts, near, codes = lax.optimization_barrier((payload, ghosts, near, codes))
+    parents = lax.all_to_all(payload, AXES[1:], split_axis=0, concat_axis=0, tiled=True)
     near = ghost_near(items, starts, ghosts, targets, near)
-    return finish(far_lists, parents, skel, transfer, leaf_basis, near, scales)
+    return finish(codes, parents, skel, transfer, leaf_basis, near, scales)
 
 
 def solution(mesh):
+    grp, sub = mesh.shape["grp"], mesh.shape["sub"]
+    sizes = (grp, RING, RING, sub // (RING * RING))
+    apart = Mesh(mesh.devices.reshape(sizes), AXES)
     split3 = P(AXES, None, None)
     in_specs = (split3,) * 6 + (P(AXES, None), P(AXES), P(AXES, None))
-    return jax.shard_map(body, mesh=mesh, in_specs=in_specs, out_specs=split3, check_vma=False)
+    return jax.shard_map(body, mesh=apart, in_specs=in_specs, out_specs=split3, check_vma=False)

time: 127 us -> 126 us (level); the launches traced: 127 us -> 123 us
  waiting for transfers between devices: 46 us -> 35.8 us
  starting transfers between devices: 19 us -> 23.2 us
    all_to_all x1, waiting for transfers between devices: 26.6 us -> 0.87 us  [body(): lax.all_to_all(packed, AXES, split_axis=0, concat_axis=0, tiled=True)]
    ppermute x0 -> x3, waiting for transfers between devices: none -> 18.9 us  [ring_copies(): lax.ppermute(payload, 'x', [(x, (x + dx) % RING) for x in range(RING)])]
    ppermute x0 -> x3, starting transfers between devices: none -> 3.75 us  [ring_copies(): lax.ppermute(payload, 'x', [(x, (x + dx) % RING) for x in range(RING)])]
    all_to_all x1, waiting for transfers between devices: 19.5 us -> 16 us  [body(): lax.all_to_all(payload, AXES[1:], split_axis=0, concat_axis=0, tiled=True)]
    pallas_call x1 -> x2, Pallas kernels: 5.81 us -> 7.03 us  [the longest x1 4.49 us: parent_payload(): pl.pallas_call(moments_kernel, out_shape=jax.ShapeDtypeStruct((80, 128),...]
  transfers between devices with their start and end apart: 2 -> 5, of which waited for: 2 -> 5; matrix products, arithmetic and copies ran while one was open for 0% -> 0% of each run, Pallas kernels for 40% -> 43%
where the time goes in v4:
time: 126 us; the launch traced here: 123 us
  Pallas kernels  62.3 us (49%)
  waiting for transfers between devices  35.8 us (28%)
  starting transfers between devices  23.2 us (18%)
    pallas_call x1, Pallas kernels, local_near(): pl.pallas_call(local_kernel, out_shape=(jax.ShapeDtypeStruct((leaves, 3,...  28.8 us
    ppermute x3, waiting for transfers between devices, ring_copies(): lax.ppermute(payload, 'x', [(x, (x + dx) % RING) for x in range(RING)])  18.9 us
    pallas_call x1, Pallas kernels, ghost_near(): pl.pallas_call(ghost_kernel, out_shape=jax.ShapeDtypeStruct(start.shape,...  16.6 us
    all_to_all x1, waiting for transfers between devices, body(): lax.all_to_all(payload, AXES[1:], split_axis=0, concat_axis=0, tiled=True)  16 us
    all_to_all x1, starting transfers between devices, body(): lax.all_to_all(packed, AXES, split_axis=0, concat_axis=0, tiled=True)  11.9 us
    all_to_all x1, starting transfers between devices, body(): lax.all_to_all(payload, AXES[1:], split_axis=0, concat_axis=0, tiled=True)  7.54 us
    pallas_call x1, Pallas kernels, finish(): pl.pallas_call(functools.partial(finish_kernel, scales=scales), out_shape...  6.12 us
    pallas_call x1, Pallas kernels, parent_payload(): pl.pallas_call(moments_kernel, out_shape=jax.ShapeDtypeStruct((80, 128),...  4.49 us
  transfers between devices with their start and end apart: 5, of which 5 were waited for; matrix products, arithmetic and copies ran while one was open for 0% of the time, Pallas kernels for 43%

profile of v4, /device:TPU:1, one launch (start us, length us, event | category | flops | bytes accessed | tf_op | source)
XLA Modules:
  0.0 123.1 jit_solution(12400154696406820067)
XLA Ops:
  0.0 3.8 %pack.1 = bf16[128,152,128]{2,1,0:T(8,128)(2,1)} custom-call(s32[4,128]{1,0:T(4,128)} %bitcast.10, bf16[3,64,256]{2,1,0:T(8,128)(2,1)} %bitcast.6, bf16[64,16,256]{2,1,0:T(8,128)(2,1)} %charges.3), custom_call_target="tpu_custom_call" | custom-call | bytes 6291456 | tf_op jit(solution)/shard_map/pack/pallas_call | solution.py:111
  3.8 0.0 copy-start.3
  3.8 11.9 %all-to-all-start = ((bf16[128,152,128]{2,1,0:T(8,128)(2,1)}), bf16[128,152,128]{2,1,0:T(8,128)(2,1)}, u32[]{:S(2)}, u32[]{:S(2)}) async-start(bf16[128,152,128]{2,1,0:T(8,128)(2,1)} %pack.1), calls=%async_computation | async-start | bytes 9961472 | tf_op jit(solution)/shard_map/all_to_all | solution.py:561
  15.7 4.5 %moments.1.refs_0_ = bf16[80,128]{1,0:T(8,128)(2,1)} custom-call(bf16[64,16,256]{2,1,0:T(8,128)(2,1)} %charges.3, bf16[64,64,256]{2,1,0:T(8,128)(2,1)} %basis_hbm.1, bf16[64,64,64]{2,1,0:T(8,128)(2,1)} %transfer_hbm.1, bf16[3,8,64]{2,1,0:T(8,128)(2,1)} %bitcast.8), custom_call_target="tpu_custom_call" | custom-call | flops 100000000 | bytes 4194304 | tf_op jit(solution)/shard_map/moments/pallas_call | solution.py:162
  20.2 2.6 %collective-permute-start.2 = (bf16[80,128]{1,0:T(8,128)(2,1)}, bf16[80,128]{1,0:T(8,128)(2,1)S(1)}, u32[]{:S(2)}, u32[]{:S(2)}) collective-permute-start(bf16[80,128]{1,0:T(8,128)(2,1)} %moments.1.refs_0_), channel_id=1, source_target_pairs={{0,96},{32,0},{64,32},{96,64},{1,97},{33,1},{65,33},{97,65},{2,98}... | collective-permute-start | bytes 61448 | tf_op jit(solution)/shard_map/ppermute | solution.py:186
  22.8 0.6 collective-permute-start.1
  23.4 0.6 collective-permute-start
  24.0 0.0 copy-done.3
  24.0 0.6 and_or_fusion.far
  24.6 28.8 %local_near.1 = (bf16[64,3,128,256]{3,2,1,0:T(8,128)(2,1)}, s32[1040]{0:T(1024)}, s32[65]{0:T(128)}, f32[64,16,256]{2,1,0:T(8,128)}) custom-call(s32[16,64]{1,0:T(8,128)} %bitcast.11, s32[64]{0:T(128)} %counts.1, bf16[3,64,256]{2,1,0:T(8,128)(2,1)} %bitcast.7, bf16[64,16,256]{2,1,0:T(8,128)(2,1)} %charges.3), custom_call_target="tpu_custom_call" | custom-call | flops 2000000000 | bytes 15728640 | tf_op jit(solution)/shard_map/local_near/pallas_call | solution.py:290
  53.4 17.3 %collective-permute-done.2.refs_3_ = bf16[80,128]{1,0:T(8,128)(2,1)S(1)} collective-permute-done((bf16[80,128]{1,0:T(8,128)(2,1)}, bf16[80,128]{1,0:T(8,128)(2,1)S(1)}, u32[]{:S(2)}, u32[]{:S(2)}) %collective-permute-start.2) | collective-permute-done | bytes 20512 | tf_op jit(solution)/shard_map/ppermute | solution.py:186
  70.7 0.0 copy-start
  70.7 1.5 %collective-permute-done.1.refs_2_ = bf16[80,128]{1,0:T(8,128)(2,1)S(1)} collective-permute-done((bf16[80,128]{1,0:T(8,128)(2,1)}, bf16[80,128]{1,0:T(8,128)(2,1)S(1)}, u32[]{:S(2)}, u32[]{:S(2)}) %collective-permute-start.1) | collective-permute-done | bytes 20512 | tf_op jit(solution)/shard_map/ppermute | solution.py:186
  72.2 0.0 copy-start.1
  72.2 0.1 collective-permute-done.refs_1_
  72.3 0.0 copy-done
  72.3 0.5 copy-done.1
  72.8 0.0 copy-start.2
  72.8 0.6 copy-done.2
  73.4 2.5 %ring_copies.1 = bf16[32,304,128]{2,1,0:T(8,128)(2,1)} custom-call(bf16[80,128]{1,0:T(8,128)(2,1)} %moments.1.refs_0_, bf16[80,128]{1,0:T(8,128)(2,1)} %copy-done.2, bf16[80,128]{1,0:T(8,128)(2,1)} %copy-done.1, bf16[80,128]{1,0:T(8,128)(2,1)} %copy-done), custom_call_target="tpu_custom_call" | custom-call | bytes 3145728 | tf_op jit(solution)/shard_map/ring_copies/pallas_call | solution.py:188
  76.0 0.9 all-to-all-done.ghosts_hbm
  76.8 7.5 %all-to-all-start.1 = ((bf16[32,304,128]{2,1,0:T(8,128)(2,1)}), bf16[32,304,128]{2,1,0:T(8,128)(2,1)}, u32[]{:S(2)}, u32[]{:S(2)}) async-start(bf16[32,304,128]{2,1,0:T(8,128)(2,1)} %ring_copies.1), calls=%async_computation.1 | async-start | bytes 4980736 | tf_op jit(solution)/shard_map/all_to_all | solution.py:568
  84.4 16.6 %ghost_near.1.near_hbm = f32[64,16,256]{2,1,0:T(8,128)} custom-call(s32[1040]{0:T(1024)} %get-tuple-element.16.items, s32[65]{0:T(128)} %get-tuple-element.17.starts, bf16[128,152,128]{2,1,0:T(8,128)(2,1)} %all-to-all-done.ghosts_hbm, bf16[64,3,128,256]{3,2,1,0:T(8,128)(2,1)} %get-tuple-element.19.targets_hbm, f32[64,16,256]{2,1,0:T(8,128)} %get-tuple-element.20.start_hbm), custom_call_target="tpu_custom_call" | custom-call | flops 10000000000 | bytes 20971520 | tf_op jit(solution)/shard_map/ghost_near/pallas_call | solution.py:387
  101.0 16.0 %all-to-all-done.1.parents = bf16[32,304,128]{2,1,0:T(8,128)(2,1)} async-done(((bf16[32,304,128]{2,1,0:T(8,128)(2,1)}), bf16[32,304,128]{2,1,0:T(8,128)(2,1)}, u32[]{:S(2)}, u32[]{:S(2)}) %all-to-all-start.1) | async-done | bytes 2490400 | tf_op jit(solution)/shard_map/all_to_all | solution.py:568
  117.0 6.1 %finish.1 = bf16[64,16,256]{2,1,0:T(8,128)(2,1)} custom-call(s32[8,27]{1,0:T(8,128)} %and_or_fusion.far, bf16[32,304,128]{2,1,0:T(8,128)(2,1)} %all-to-all-done.1.parents, bf16[3,8,64]{2,1,0:T(8,128)(2,1)} %bitcast.9, bf16[64,64,64]{2,1,0:T(8,128)(2,1)} %transfer_hbm.1, bf16[64,64,256]{2,1,0:T(8,128)(2,1)} %basis_hbm.1, f32[64,16,256]{2,1,0:T(8,128)} %ghost_near.1.near_hbm), custom_call_target="tpu_custom_call" | custom-call | flops 100000000 | bytes 8388608 | tf_op jit(solution)/shard_map/finish/pallas_call | solution.py:517
Async XLA Ops:
  3.8 20.2 %copy-start.3 = (s32[8,27]{1,0:T(8,128)S(1)}, s32[8,27]{1,0:T(8,128)}, u32[]{:S(2)}) copy-start(s32[8,27]{1,0:T(8,128)} %param.17) | copy-start | bytes 2596
  3.8 73.0 %all-to-all-start = ((bf16[128,152,128]{2,1,0:T(8,128)(2,1)}), bf16[128,152,128]{2,1,0:T(8,128)(2,1)}, u32[]{:S(2)}, u32[]{:S(2)}) async-start(bf16[128,152,128]{2,1,0:T(8,128)(2,1)} %pack.1), calls=%async_computation | async-start | bytes 9961472 | tf_op jit(solution)/shard_map/all_to_all | solution.py:561
  20.2 50.5 %collective-permute-start.2 = (bf16[80,128]{1,0:T(8,128)(2,1)}, bf16[80,128]{1,0:T(8,128)(2,1)S(1)}, u32[]{:S(2)}, u32[]{:S(2)}) collective-permute-start(bf16[80,128]{1,0:T(8,128)(2,1)} %moments.1.refs_0_), channel_id=1, source_target_pairs={{0,96},{32,0},{64,32},{96,64},{1,97},{33,1},{65,33},{97,65},{2,98}... | collective-permute-start | bytes 61448 | tf_op jit(solution)/shard_map/ppermute | solution.py:186
  22.8 49.4 %collective-permute-start.1 = (bf16[80,128]{1,0:T(8,128)(2,1)}, bf16[80,128]{1,0:T(8,128)(2,1)S(1)}, u32[]{:S(2)}, u32[]{:S(2)}) collective-permute-start(bf16[80,128]{1,0:T(8,128)(2,1)} %moments.1.refs_0_), channel_id=1, source_target_pairs={{0,64},{32,96},{64,0},{96,32},{1,65},{33,97},{65,1},{97,33},{2,66}... | collective-permute-start | bytes 61448 | tf_op jit(solution)/shard_map/ppermute | solution.py:186
  23.4 48.9 %collective-permute-start = (bf16[80,128]{1,0:T(8,128)(2,1)}, bf16[80,128]{1,0:T(8,128)(2,1)S(1)}, u32[]{:S(2)}, u32[]{:S(2)}) collective-permute-start(bf16[80,128]{1,0:T(8,128)(2,1)} %moments.1.refs_0_), channel_id=1, source_target_pairs={{0,32},{32,64},{64,96},{96,0},{1,33},{33,65},{65,97},{97,1},{2,34}... | collective-permute-start | bytes 61448 | tf_op jit(solution)/shard_map/ppermute | solution.py:186
  70.7 1.6 %copy-start = (bf16[80,128]{1,0:T(8,128)(2,1)}, bf16[80,128]{1,0:T(8,128)(2,1)S(1)}, u32[]{:S(2)}) copy-start(bf16[80,128]{1,0:T(8,128)(2,1)S(1)} %collective-permute-done.2.refs_3_) | copy-start | bytes 61444
  72.2 0.6 copy-start.1
  72.8 0.6 copy-start.2
  76.8 40.1 %all-to-all-start.1 = ((bf16[32,304,128]{2,1,0:T(8,128)(2,1)}), bf16[32,304,128]{2,1,0:T(8,128)(2,1)}, u32[]{:S(2)}, u32[]{:S(2)}) async-start(bf16[32,304,128]{2,1,0:T(8,128)(2,1)} %ring_copies.1), calls=%async_computation.1 | async-start | bytes 4980736 | tf_op jit(solution)/shard_map/all_to_all | solution.py:568

commit v5 on v4

--- a/solution.py
+++ b/solution.py
@@ -17,7 +17,7 @@
 MIB = 1024 * 1024
 VMEM_LIMIT = 62 * MIB
 GROUP = 8
-UNROLL = 16
+UNROLL = 32
 
 SMEM = pl.BlockSpec(memory_space=pltpu.SMEM)
 VMEM = pl.BlockSpec(memory_space=pltpu.VMEM)
@@ -314,7 +314,19 @@
 
 
 def ghost_kernel(
-    items, starts, ghosts_hbm, targets_hbm, start_hbm, near_hbm, ghosts, targets, table, acc, sems
+    items_hbm,
+    starts_hbm,
+    ghosts_hbm,
+    targets_hbm,
+    start_hbm,
+    near_hbm,
+    ghosts,
+    targets,
+    table,
+    acc,
+    items,
+    starts,
+    sems,
 ):
     leaves = start_hbm.shape[0]
     part = leaves // PARTS
@@ -335,6 +347,8 @@
     for q in range(PARTS):
         arrival(q).start()
     begin = fetch(start_hbm, acc.at[pl.ds(0, leaves)], sems.at[3, 0])
+    listed = fetch(items_hbm, items, sems.at[3, 1])
+    bounds = fetch(starts_hbm, starts, sems.at[3, 2])
     piece(0).start()
     acc[leaves] = jnp.zeros(acc.shape[1:], F32)
 
@@ -350,6 +364,8 @@
 
     lax.fori_loop(0, PARTS, arrived, 0)
     begin.wait()
+    listed.wait()
+    bounds.wait()
     for q in range(1, PARTS):
         piece(q).start()
 
@@ -387,13 +403,15 @@
     return pl.pallas_call(
         ghost_kernel,
         out_shape=jax.ShapeDtypeStruct(start.shape, F32),
-        in_specs=[SMEM, SMEM, HBM, HBM, HBM],
+        in_specs=[HBM, HBM, HBM, HBM, HBM],
         out_specs=HBM,
         scratch_shapes=[
             pltpu.VMEM(ghosts.shape, BF16),
             pltpu.VMEM(targets.shape, BF16),
             pltpu.VMEM((devices * 24, 128), F32),
             pltpu.VMEM((leaves + 1, rhs, points), F32),
+            pltpu.SMEM(items.shape, I32),
+            pltpu.SMEM(starts.shape, I32),
             pltpu.SemaphoreType.DMA((4, PARTS)),
         ],
         compiler_params=pltpu.CompilerParams(vmem_limit_bytes=VMEM_LIMIT),

time: 126 us -> 125 us (level)
  waiting for transfers between devices: 35.8 us -> 39.4 us
  Pallas kernels: 62.3 us -> 58.7 us
    all_to_all x1, waiting for transfers between devices: 16 us -> 19.2 us  [body(): lax.all_to_all(payload, AXES[1:], split_axis=0, concat_axis=0, tiled=True)]
    pallas_call x1, Pallas kernels: 16.6 us -> 13.4 us  [ghost_near(): pl.pallas_call(ghost_kernel, out_shape=jax.ShapeDtypeStruct(start.shape,...]
  transfers between devices with their start and end apart: 5 -> 5, of which waited for: 5 -> 5; matrix products, arithmetic and copies ran while one was open for 0% -> 0% of each run, Pallas kernels for 43% -> 40%
where the time goes in v5:
time: 125 us; the launch traced here: 123 us
  Pallas kernels  58.7 us (47%)
  waiting for transfers between devices  39.4 us (32%)
  starting transfers between devices  23.2 us (19%)
    pallas_call x1, Pallas kernels, local_near(): pl.pallas_call(local_kernel, out_shape=(jax.ShapeDtypeStruct((leaves, 3,...  28.4 us
    ppermute x3, waiting for transfers between devices, ring_copies(): lax.ppermute(payload, 'x', [(x, (x + dx) % RING) for x in range(RING)])  19.3 us
    all_to_all x1, waiting for transfers between devices, body(): lax.all_to_all(payload, AXES[1:], split_axis=0, concat_axis=0, tiled=True)  19.2 us
    pallas_call x1, Pallas kernels, ghost_near(): pl.pallas_call(ghost_kernel, out_shape=jax.ShapeDtypeStruct(start.shape,...  13.4 us
    all_to_all x1, starting transfers between devices, body(): lax.all_to_all(packed, AXES, split_axis=0, concat_axis=0, tiled=True)  11.9 us
    all_to_all x1, starting transfers between devices, body(): lax.all_to_all(payload, AXES[1:], split_axis=0, concat_axis=0, tiled=True)  7.54 us
    pallas_call x1, Pallas kernels, finish(): pl.pallas_call(functools.partial(finish_kernel, scales=scales), out_shape...  6.11 us
    pallas_call x1, Pallas kernels, parent_payload(): pl.pallas_call(moments_kernel, out_shape=jax.ShapeDtypeStruct((80, 128),...  4.49 us
  transfers between devices with their start and end apart: 5, of which 5 were waited for; matrix products, arithmetic and copies ran while one was open for 0% of the time, Pallas kernels for 40%

profile of v5, /device:TPU:1, one launch (start us, length us, event | category | flops | bytes accessed | tf_op | source)
XLA Modules:
  0.0 123.1 jit_solution(10406194001114205389)
XLA Ops:
  0.0 3.8 %pack.1 = bf16[128,152,128]{2,1,0:T(8,128)(2,1)} custom-call(s32[4,128]{1,0:T(4,128)} %bitcast.10, bf16[3,64,256]{2,1,0:T(8,128)(2,1)} %bitcast.6, bf16[64,16,256]{2,1,0:T(8,128)(2,1)} %charges.3), custom_call_target="tpu_custom_call" | custom-call | bytes 6291456 | tf_op jit(solution)/shard_map/pack/pallas_call | solution.py:111
  3.8 0.0 copy-start.3
  3.8 11.9 %all-to-all-start = ((bf16[128,152,128]{2,1,0:T(8,128)(2,1)}), bf16[128,152,128]{2,1,0:T(8,128)(2,1)}, u32[]{:S(2)}, u32[]{:S(2)}) async-start(bf16[128,152,128]{2,1,0:T(8,128)(2,1)} %pack.1), calls=%async_computation | async-start | bytes 9961472 | tf_op jit(solution)/shard_map/all_to_all | solution.py:579
  15.7 4.5 %moments.1.refs_0_ = bf16[80,128]{1,0:T(8,128)(2,1)} custom-call(bf16[64,16,256]{2,1,0:T(8,128)(2,1)} %charges.3, bf16[64,64,256]{2,1,0:T(8,128)(2,1)} %basis_hbm.1, bf16[64,64,64]{2,1,0:T(8,128)(2,1)} %transfer_hbm.1, bf16[3,8,64]{2,1,0:T(8,128)(2,1)} %bitcast.8), custom_call_target="tpu_custom_call" | custom-call | flops 100000000 | bytes 4194304 | tf_op jit(solution)/shard_map/moments/pallas_call | solution.py:162
  20.2 2.6 %collective-permute-start.2 = (bf16[80,128]{1,0:T(8,128)(2,1)}, bf16[80,128]{1,0:T(8,128)(2,1)S(1)}, u32[]{:S(2)}, u32[]{:S(2)}) collective-permute-start(bf16[80,128]{1,0:T(8,128)(2,1)} %moments.1.refs_0_), channel_id=1, source_target_pairs={{0,96},{32,0},{64,32},{96,64},{1,97},{33,1},{65,33},{97,65},{2,98}... | collective-permute-start | bytes 61448 | tf_op jit(solution)/shard_map/ppermute | solution.py:186
  22.8 0.6 collective-permute-start.1
  23.4 0.6 collective-permute-start
  24.0 0.0 copy-done.3
  24.0 0.6 and_or_fusion.far
  24.6 28.4 %local_near.1 = (bf16[64,3,128,256]{3,2,1,0:T(8,128)(2,1)}, s32[1056]{0:T(1024)}, s32[65]{0:T(128)}, f32[64,16,256]{2,1,0:T(8,128)}) custom-call(s32[16,64]{1,0:T(8,128)} %bitcast.11, s32[64]{0:T(128)} %counts.1, bf16[3,64,256]{2,1,0:T(8,128)(2,1)} %bitcast.7, bf16[64,16,256]{2,1,0:T(8,128)(2,1)} %charges.3), custom_call_target="tpu_custom_call" | custom-call | flops 2000000000 | bytes 15728640 | tf_op jit(solution)/shard_map/local_near/pallas_call | solution.py:290
  53.0 17.7 %collective-permute-done.2.refs_3_ = bf16[80,128]{1,0:T(8,128)(2,1)S(1)} collective-permute-done((bf16[80,128]{1,0:T(8,128)(2,1)}, bf16[80,128]{1,0:T(8,128)(2,1)S(1)}, u32[]{:S(2)}, u32[]{:S(2)}) %collective-permute-start.2) | collective-permute-done | bytes 20512 | tf_op jit(solution)/shard_map/ppermute | solution.py:186
  70.7 0.0 copy-start
  70.7 1.5 %collective-permute-done.1.refs_2_ = bf16[80,128]{1,0:T(8,128)(2,1)S(1)} collective-permute-done((bf16[80,128]{1,0:T(8,128)(2,1)}, bf16[80,128]{1,0:T(8,128)(2,1)S(1)}, u32[]{:S(2)}, u32[]{:S(2)}) %collective-permute-start.1) | collective-permute-done | bytes 20512 | tf_op jit(solution)/shard_map/ppermute | solution.py:186
  72.2 0.0 copy-start.1
  72.2 0.1 collective-permute-done.refs_1_
  72.3 0.0 copy-done
  72.3 0.5 copy-done.1
  72.8 0.0 copy-start.2
  72.8 0.6 copy-done.2
  73.4 2.5 %ring_copies.1 = bf16[32,304,128]{2,1,0:T(8,128)(2,1)} custom-call(bf16[80,128]{1,0:T(8,128)(2,1)} %moments.1.refs_0_, bf16[80,128]{1,0:T(8,128)(2,1)} %copy-done.2, bf16[80,128]{1,0:T(8,128)(2,1)} %copy-done.1, bf16[80,128]{1,0:T(8,128)(2,1)} %copy-done), custom_call_target="tpu_custom_call" | custom-call | bytes 3145728 | tf_op jit(solution)/shard_map/ring_copies/pallas_call | solution.py:188
  76.0 0.9 all-to-all-done.ghosts_hbm
  76.8 7.5 %all-to-all-start.1 = ((bf16[32,304,128]{2,1,0:T(8,128)(2,1)}), bf16[32,304,128]{2,1,0:T(8,128)(2,1)}, u32[]{:S(2)}, u32[]{:S(2)}) async-start(bf16[32,304,128]{2,1,0:T(8,128)(2,1)} %ring_copies.1), calls=%async_computation.1 | async-start | bytes 4980736 | tf_op jit(solution)/shard_map/all_to_all | solution.py:586
  84.4 13.4 %ghost_near.1.near_hbm = f32[64,16,256]{2,1,0:T(8,128)} custom-call(s32[1056]{0:T(1024)} %get-tuple-element.16.items_hbm, s32[65]{0:T(128)} %get-tuple-element.17.starts_hbm, bf16[128,152,128]{2,1,0:T(8,128)(2,1)} %all-to-all-done.ghosts_hbm, bf16[64,3,128,256]{3,2,1,0:T(8,128)(2,1)} %get-tuple-element.19.targets_hbm, f32[64,16,256]{2,1,0:T(8,128)} %get-tuple-element.20.start_hbm), custom_call_target="tpu_custom_call" | custom-call | flops 10000000000 | bytes 20971520 | tf_op jit(solution)/shard_map/ghost_near/pallas_call | solution.py:403
  97.7 19.2 %all-to-all-done.1.parents = bf16[32,304,128]{2,1,0:T(8,128)(2,1)} async-done(((bf16[32,304,128]{2,1,0:T(8,128)(2,1)}), bf16[32,304,128]{2,1,0:T(8,128)(2,1)}, u32[]{:S(2)}, u32[]{:S(2)}) %all-to-all-start.1) | async-done | bytes 2490400 | tf_op jit(solution)/shard_map/all_to_all | solution.py:586
  117.0 6.1 %finish.1 = bf16[64,16,256]{2,1,0:T(8,128)(2,1)} custom-call(s32[8,27]{1,0:T(8,128)} %and_or_fusion.far, bf16[32,304,128]{2,1,0:T(8,128)(2,1)} %all-to-all-done.1.parents, bf16[3,8,64]{2,1,0:T(8,128)(2,1)} %bitcast.9, bf16[64,64,64]{2,1,0:T(8,128)(2,1)} %transfer_hbm.1, bf16[64,64,256]{2,1,0:T(8,128)(2,1)} %basis_hbm.1, f32[64,16,256]{2,1,0:T(8,128)} %ghost_near.1.near_hbm), custom_call_target="tpu_custom_call" | custom-call | flops 100000000 | bytes 8388608 | tf_op jit(solution)/shard_map/finish/pallas_call | solution.py:535
Async XLA Ops:
  3.8 20.2 %copy-start.3 = (s32[8,27]{1,0:T(8,128)S(1)}, s32[8,27]{1,0:T(8,128)}, u32[]{:S(2)}) copy-start(s32[8,27]{1,0:T(8,128)} %param.17) | copy-start | bytes 2596
  3.8 73.0 %all-to-all-start = ((bf16[128,152,128]{2,1,0:T(8,128)(2,1)}), bf16[128,152,128]{2,1,0:T(8,128)(2,1)}, u32[]{:S(2)}, u32[]{:S(2)}) async-start(bf16[128,152,128]{2,1,0:T(8,128)(2,1)} %pack.1), calls=%async_computation | async-start | bytes 9961472 | tf_op jit(solution)/shard_map/all_to_all | solution.py:579
  20.2 50.5 %collective-permute-start.2 = (bf16[80,128]{1,0:T(8,128)(2,1)}, bf16[80,128]{1,0:T(8,128)(2,1)S(1)}, u32[]{:S(2)}, u32[]{:S(2)}) collective-permute-start(bf16[80,128]{1,0:T(8,128)(2,1)} %moments.1.refs_0_), channel_id=1, source_target_pairs={{0,96},{32,0},{64,32},{96,64},{1,97},{33,1},{65,33},{97,65},{2,98}... | collective-permute-start | bytes 61448 | tf_op jit(solution)/shard_map/ppermute | solution.py:186
  22.8 49.4 %collective-permute-start.1 = (bf16[80,128]{1,0:T(8,128)(2,1)}, bf16[80,128]{1,0:T(8,128)(2,1)S(1)}, u32[]{:S(2)}, u32[]{:S(2)}) collective-permute-start(bf16[80,128]{1,0:T(8,128)(2,1)} %moments.1.refs_0_), channel_id=1, source_target_pairs={{0,64},{32,96},{64,0},{96,32},{1,65},{33,97},{65,1},{97,33},{2,66}... | collective-permute-start | bytes 61448 | tf_op jit(solution)/shard_map/ppermute | solution.py:186
  23.4 48.9 %collective-permute-start = (bf16[80,128]{1,0:T(8,128)(2,1)}, bf16[80,128]{1,0:T(8,128)(2,1)S(1)}, u32[]{:S(2)}, u32[]{:S(2)}) collective-permute-start(bf16[80,128]{1,0:T(8,128)(2,1)} %moments.1.refs_0_), channel_id=1, source_target_pairs={{0,32},{32,64},{64,96},{96,0},{1,33},{33,65},{65,97},{97,1},{2,34}... | collective-permute-start | bytes 61448 | tf_op jit(solution)/shard_map/ppermute | solution.py:186
  70.7 1.6 %copy-start = (bf16[80,128]{1,0:T(8,128)(2,1)}, bf16[80,128]{1,0:T(8,128)(2,1)S(1)}, u32[]{:S(2)}) copy-start(bf16[80,128]{1,0:T(8,128)(2,1)S(1)} %collective-permute-done.2.refs_3_) | copy-start | bytes 61444
  72.2 0.6 copy-start.1
  72.8 0.6 copy-start.2
  76.8 40.1 %all-to-all-start.1 = ((bf16[32,304,128]{2,1,0:T(8,128)(2,1)}), bf16[32,304,128]{2,1,0:T(8,128)(2,1)}, u32[]{:S(2)}, u32[]{:S(2)}) async-start(bf16[32,304,128]{2,1,0:T(8,128)(2,1)} %ring_copies.1), calls=%async_computation.1 | async-start | bytes 4980736 | tf_op jit(solution)/shard_map/all_to_all | solution.py:586

commit v6 on v5

--- a/solution.py
+++ b/solution.py
@@ -195,7 +195,7 @@
             pltpu.VMEM((304, lanes), BF16),
             pltpu.SemaphoreType.DMA((groups,)),
         ],
-        compiler_params=pltpu.CompilerParams(vmem_limit_bytes=VMEM_LIMIT),
+        compiler_params=pltpu.CompilerParams(vmem_limit_bytes=16 * MIB),
         cost_estimate=pl.CostEstimate(flops=0, bytes_accessed=3 * MIB, transcendentals=0),
         name="ring_copies",
     )(*pieces)

time: 125 us -> 123 us (0.984)
  waiting for transfers between devices: 39.4 us -> 45.2 us
  Pallas kernels: 58.7 us -> 54.1 us
  starting transfers between devices: 23.2 us -> 21.7 us
    all_to_all x1, waiting for transfers between devices: 19.2 us -> 23.1 us  [body(): lax.all_to_all(payload, AXES[1:], split_axis=0, concat_axis=0, tiled=True)]
    pallas_call x1, Pallas kernels: 13.4 us -> 9.51 us  [ghost_near(): pl.pallas_call(ghost_kernel, out_shape=jax.ShapeDtypeStruct(start.shape,...]
    all_to_all x1, waiting for transfers between devices: 0.87 us -> 2.78 us  [body(): lax.all_to_all(packed, AXES, split_axis=0, concat_axis=0, tiled=True)]
    all_to_all x1, starting transfers between devices: 7.54 us -> 6 us  [body(): lax.all_to_all(payload, AXES[1:], split_axis=0, concat_axis=0, tiled=True)]
  transfers between devices with their start and end apart: 5 -> 5, of which waited for: 5 -> 5; matrix products, arithmetic and copies ran while one was open for 0% -> 0% of each run, Pallas kernels for 40% -> 36%
where the time goes in v6:
time: 123 us; the launch traced here: 122 us
  Pallas kernels  54.1 us (44%)
  waiting for transfers between devices  45.2 us (37%)
  starting transfers between devices  21.7 us (18%)
    pallas_call x1, Pallas kernels, local_near(): pl.pallas_call(local_kernel, out_shape=(jax.ShapeDtypeStruct((leaves, 3,...  28.4 us
    all_to_all x1, waiting for transfers between devices, body(): lax.all_to_all(payload, AXES[1:], split_axis=0, concat_axis=0, tiled=True)  23.1 us
    ppermute x3, waiting for transfers between devices, ring_copies(): lax.ppermute(payload, 'x', [(x, (x + dx) % RING) for x in range(RING)])  19.3 us
    all_to_all x1, starting transfers between devices, body(): lax.all_to_all(packed, AXES, split_axis=0, concat_axis=0, tiled=True)  11.9 us
    pallas_call x1, Pallas kernels, ghost_near(): pl.pallas_call(ghost_kernel, out_shape=jax.ShapeDtypeStruct(start.shape,...  9.51 us
    pallas_call x1, Pallas kernels, finish(): pl.pallas_call(functools.partial(finish_kernel, scales=scales), out_shape...  6.12 us
    all_to_all x1, starting transfers between devices, body(): lax.all_to_all(payload, AXES[1:], split_axis=0, concat_axis=0, tiled=True)  6 us
    pallas_call x1, Pallas kernels, parent_payload(): pl.pallas_call(moments_kernel, out_shape=jax.ShapeDtypeStruct((80, 128),...  4.49 us
  transfers between devices with their start and end apart: 5, of which 5 were waited for; matrix products, arithmetic and copies ran while one was open for 0% of the time, Pallas kernels for 36%

profile of v6, /device:TPU:1, one launch (start us, length us, event | category | flops | bytes accessed | tf_op | source)
XLA Modules:
  0.0 121.6 jit_solution(12373701159523752978)
XLA Ops:
  0.0 3.8 %pack.1 = bf16[128,152,128]{2,1,0:T(8,128)(2,1)} custom-call(s32[4,128]{1,0:T(4,128)} %bitcast.10, bf16[3,64,256]{2,1,0:T(8,128)(2,1)} %bitcast.6, bf16[64,16,256]{2,1,0:T(8,128)(2,1)} %charges.3), custom_call_target="tpu_custom_call" | custom-call | bytes 6291456 | tf_op jit(solution)/shard_map/pack/pallas_call | solution.py:111
  3.8 0.0 copy-start.1
  3.8 11.9 %all-to-all-start = ((bf16[128,152,128]{2,1,0:T(8,128)(2,1)}), bf16[128,152,128]{2,1,0:T(8,128)(2,1)}, u32[]{:S(2)}, u32[]{:S(2)}) async-start(bf16[128,152,128]{2,1,0:T(8,128)(2,1)} %pack.1), calls=%async_computation | async-start | bytes 9961472 | tf_op jit(solution)/shard_map/all_to_all | solution.py:579
  15.7 4.5 %moments.1.refs_0_ = bf16[80,128]{1,0:T(8,128)(2,1)} custom-call(bf16[64,16,256]{2,1,0:T(8,128)(2,1)} %charges.3, bf16[64,64,256]{2,1,0:T(8,128)(2,1)} %basis_hbm.1, bf16[64,64,64]{2,1,0:T(8,128)(2,1)} %transfer_hbm.1, bf16[3,8,64]{2,1,0:T(8,128)(2,1)} %bitcast.8), custom_call_target="tpu_custom_call" | custom-call | flops 100000000 | bytes 4194304 | tf_op jit(solution)/shard_map/moments/pallas_call | solution.py:162
  20.2 2.6 %collective-permute-start.2 = (bf16[80,128]{1,0:T(8,128)(2,1)}, bf16[80,128]{1,0:T(8,128)(2,1)S(1)}, u32[]{:S(2)}, u32[]{:S(2)}) collective-permute-start(bf16[80,128]{1,0:T(8,128)(2,1)} %moments.1.refs_0_), channel_id=1, source_target_pairs={{0,96},{32,0},{64,32},{96,64},{1,97},{33,1},{65,33},{97,65},{2,98}... | collective-permute-start | bytes 61448 | tf_op jit(solution)/shard_map/ppermute | solution.py:186
  22.8 0.6 collective-permute-start.1
  23.4 0.6 collective-permute-start
  24.0 0.0 copy-done.1
  24.0 0.6 and_or_fusion.far
  24.6 0.0 copy-start
  24.6 28.4 %local_near.1 = (bf16[64,3,128,256]{3,2,1,0:T(8,128)(2,1)}, s32[1056]{0:T(1024)}, s32[65]{0:T(128)}, f32[64,16,256]{2,1,0:T(8,128)}) custom-call(s32[16,64]{1,0:T(8,128)} %bitcast.11, s32[64]{0:T(128)} %counts.1, bf16[3,64,256]{2,1,0:T(8,128)(2,1)} %bitcast.7, bf16[64,16,256]{2,1,0:T(8,128)(2,1)} %charges.3), custom_call_target="tpu_custom_call" | custom-call | flops 2000000000 | bytes 15728640 | tf_op jit(solution)/shard_map/local_near/pallas_call | solution.py:290
  53.0 17.7 %collective-permute-done.2.refs_3_ = bf16[80,128]{1,0:T(8,128)(2,1)S(1)} collective-permute-done((bf16[80,128]{1,0:T(8,128)(2,1)}, bf16[80,128]{1,0:T(8,128)(2,1)S(1)}, u32[]{:S(2)}, u32[]{:S(2)}) %collective-permute-start.2) | collective-permute-done | bytes 20512 | tf_op jit(solution)/shard_map/ppermute | solution.py:186
  70.7 1.5 %collective-permute-done.1.refs_2_ = bf16[80,128]{1,0:T(8,128)(2,1)S(1)} collective-permute-done((bf16[80,128]{1,0:T(8,128)(2,1)}, bf16[80,128]{1,0:T(8,128)(2,1)S(1)}, u32[]{:S(2)}, u32[]{:S(2)}) %collective-permute-start.1) | collective-permute-done | bytes 20512 | tf_op jit(solution)/shard_map/ppermute | solution.py:186
  72.2 0.1 collective-permute-done.refs_1_
  72.3 0.0 copy-done
  72.3 1.8 %ring_copies.1 = bf16[32,304,128]{2,1,0:T(8,128)(2,1)} custom-call(bf16[80,128]{1,0:T(8,128)(2,1)S(1)} %copy-done, bf16[80,128]{1,0:T(8,128)(2,1)S(1)} %collective-permute-done.refs_1_, bf16[80,128]{1,0:T(8,128)(2,1)S(1)} %collective-permute-done.1.refs_2_, bf16[80,128]{1,0:T(8,128)(2,1)S(1)} %collective-permute-done.2.refs_3_), custom_call_target="tpu_custom_call" | custom-call | bytes 3145728 | tf_op jit(solution)/shard_map/ring_copies/pallas_call | solution.py:188
  74.1 2.8 %all-to-all-done.ghosts_hbm = bf16[128,152,128]{2,1,0:T(8,128)(2,1)} async-done(((bf16[128,152,128]{2,1,0:T(8,128)(2,1)}), bf16[128,152,128]{2,1,0:T(8,128)(2,1)}, u32[]{:S(2)}, u32[]{:S(2)}) %all-to-all-start) | async-done | bytes 4980768 | tf_op jit(solution)/shard_map/all_to_all | solution.py:579
  76.8 6.0 %all-to-all-start.1 = ((bf16[32,304,128]{2,1,0:T(8,128)(2,1)}), bf16[32,304,128]{2,1,0:T(8,128)(2,1)}, u32[]{:S(2)}, u32[]{:S(2)}) async-start(bf16[32,304,128]{2,1,0:T(8,128)(2,1)} %ring_copies.1), calls=%async_computation.1 | async-start | bytes 4980736 | tf_op jit(solution)/shard_map/all_to_all | solution.py:586
  82.8 9.5 %ghost_near.1.near_hbm = f32[64,16,256]{2,1,0:T(8,128)} custom-call(s32[1056]{0:T(1024)} %get-tuple-element.16.items_hbm, s32[65]{0:T(128)} %get-tuple-element.17.starts_hbm, bf16[128,152,128]{2,1,0:T(8,128)(2,1)} %all-to-all-done.ghosts_hbm, bf16[64,3,128,256]{3,2,1,0:T(8,128)(2,1)} %get-tuple-element.19.targets_hbm, f32[64,16,256]{2,1,0:T(8,128)} %get-tuple-element.20.start_hbm), custom_call_target="tpu_custom_call" | custom-call | flops 10000000000 | bytes 20971520 | tf_op jit(solution)/shard_map/ghost_near/pallas_call | solution.py:403
  92.4 23.1 %all-to-all-done.1.parents = bf16[32,304,128]{2,1,0:T(8,128)(2,1)} async-done(((bf16[32,304,128]{2,1,0:T(8,128)(2,1)}), bf16[32,304,128]{2,1,0:T(8,128)(2,1)}, u32[]{:S(2)}, u32[]{:S(2)}) %all-to-all-start.1) | async-done | bytes 2490400 | tf_op jit(solution)/shard_map/all_to_all | solution.py:586
  115.5 6.1 %finish.1 = bf16[64,16,256]{2,1,0:T(8,128)(2,1)} custom-call(s32[8,27]{1,0:T(8,128)} %and_or_fusion.far, bf16[32,304,128]{2,1,0:T(8,128)(2,1)} %all-to-all-done.1.parents, bf16[3,8,64]{2,1,0:T(8,128)(2,1)} %bitcast.9, bf16[64,64,64]{2,1,0:T(8,128)(2,1)} %transfer_hbm.1, bf16[64,64,256]{2,1,0:T(8,128)(2,1)} %basis_hbm.1, f32[64,16,256]{2,1,0:T(8,128)} %ghost_near.1.near_hbm), custom_call_target="tpu_custom_call" | custom-call | flops 100000000 | bytes 8388608 | tf_op jit(solution)/shard_map/finish/pallas_call | solution.py:535
Async XLA Ops:
  3.8 20.2 %copy-start.1 = (s32[8,27]{1,0:T(8,128)S(1)}, s32[8,27]{1,0:T(8,128)}, u32[]{:S(2)}) copy-start(s32[8,27]{1,0:T(8,128)} %param.17) | copy-start | bytes 2596
  3.8 73.0 %all-to-all-start = ((bf16[128,152,128]{2,1,0:T(8,128)(2,1)}), bf16[128,152,128]{2,1,0:T(8,128)(2,1)}, u32[]{:S(2)}, u32[]{:S(2)}) async-start(bf16[128,152,128]{2,1,0:T(8,128)(2,1)} %pack.1), calls=%async_computation | async-start | bytes 9961472 | tf_op jit(solution)/shard_map/all_to_all | solution.py:579
  20.2 50.5 %collective-permute-start.2 = (bf16[80,128]{1,0:T(8,128)(2,1)}, bf16[80,128]{1,0:T(8,128)(2,1)S(1)}, u32[]{:S(2)}, u32[]{:S(2)}) collective-permute-start(bf16[80,128]{1,0:T(8,128)(2,1)} %moments.1.refs_0_), channel_id=1, source_target_pairs={{0,96},{32,0},{64,32},{96,64},{1,97},{33,1},{65,33},{97,65},{2,98}... | collective-permute-start | bytes 61448 | tf_op jit(solution)/shard_map/ppermute | solution.py:186
  22.8 49.4 %collective-permute-start.1 = (bf16[80,128]{1,0:T(8,128)(2,1)}, bf16[80,128]{1,0:T(8,128)(2,1)S(1)}, u32[]{:S(2)}, u32[]{:S(2)}) collective-permute-start(bf16[80,128]{1,0:T(8,128)(2,1)} %moments.1.refs_0_), channel_id=1, source_target_pairs={{0,64},{32,96},{64,0},{96,32},{1,65},{33,97},{65,1},{97,33},{2,66}... | collective-permute-start | bytes 61448 | tf_op jit(solution)/shard_map/ppermute | solution.py:186
  23.4 48.9 %collective-permute-start = (bf16[80,128]{1,0:T(8,128)(2,1)}, bf16[80,128]{1,0:T(8,128)(2,1)S(1)}, u32[]{:S(2)}, u32[]{:S(2)}) collective-permute-start(bf16[80,128]{1,0:T(8,128)(2,1)} %moments.1.refs_0_), channel_id=1, source_target_pairs={{0,32},{32,64},{64,96},{96,0},{1,33},{33,65},{65,97},{97,1},{2,34}... | collective-permute-start | bytes 61448 | tf_op jit(solution)/shard_map/ppermute | solution.py:186
  24.6 47.7 %copy-start = (bf16[80,128]{1,0:T(8,128)(2,1)S(1)}, bf16[80,128]{1,0:T(8,128)(2,1)}, u32[]{:S(2)}) copy-start(bf16[80,128]{1,0:T(8,128)(2,1)} %moments.1.refs_0_) | copy-start | bytes 61444
  76.8 38.7 %all-to-all-start.1 = ((bf16[32,304,128]{2,1,0:T(8,128)(2,1)}), bf16[32,304,128]{2,1,0:T(8,128)(2,1)}, u32[]{:S(2)}, u32[]{:S(2)}) async-start(bf16[32,304,128]{2,1,0:T(8,128)(2,1)} %ring_copies.1), calls=%async_computation.1 | async-start | bytes 4980736 | tf_op jit(solution)/shard_map/all_to_all | solution.py:586

commit v7 on v6

--- a/solution.py
+++ b/solution.py
@@ -84,7 +84,7 @@
         out[e, 128:152, :] = jnp.concatenate(six, axis=0).astype(BF16)
 
     def four(e):
-        for n in range(4):
+        for n in range(8):
             one(e + n)
         return 0
 
@@ -96,7 +96,7 @@
         return pltpu.make_async_copy(out.at[span], out_hbm.at[span], sems.at[3 + q])
 
     def some(q, _):
-        lax.fori_loop(0, size // 4, lambda n, _: four(q * size + 4 * n), 0)
+        lax.fori_loop(0, size // 8, lambda n, _: four(q * size + 8 * n), 0)
         piece(q).start()
         return 0
 
@@ -498,7 +498,7 @@
         local[p] = (far_scale * total).astype(BF16)
         return 0
 
-    lax.fori_loop(0, clusters, coefficients, 0, unroll=2)
+    lax.fori_loop(0, clusters, coefficients, 0, unroll=4)
 
     for copy in fetches:
         copy.wait()

time: 123 us -> 121 us (0.984); the launches traced: 122 us -> 121 us
  waiting for transfers between devices: 45.2 us -> 41.9 us
  Pallas kernels: 54.1 us -> 56.9 us
    all_to_all x1, waiting for transfers between devices: 23.1 us -> 19.8 us  [body(): lax.all_to_all(payload, AXES[1:], split_axis=0, concat_axis=0, tiled=True)]
    pallas_call x1, Pallas kernels: 9.51 us -> 12.8 us  [ghost_near(): pl.pallas_call(ghost_kernel, out_shape=jax.ShapeDtypeStruct(start.shape,...]
  transfers between devices with their start and end apart: 5 -> 5, of which waited for: 5 -> 5; matrix products, arithmetic and copies ran while one was open for 0% -> 0% of each run, Pallas kernels for 36% -> 39%
where the time goes in v7:
time: 121 us
  Pallas kernels  56.9 us (47%)
  waiting for transfers between devices  41.9 us (35%)
  starting transfers between devices  21.7 us (18%)
    pallas_call x1, Pallas kernels, local_near(): pl.pallas_call(local_kernel, out_shape=(jax.ShapeDtypeStruct((leaves, 3,...  28.4 us
    all_to_all x1, waiting for transfers between devices, body(): lax.all_to_all(payload, AXES[1:], split_axis=0, concat_axis=0, tiled=True)  19.8 us
    ppermute x3, waiting for transfers between devices, ring_copies(): lax.ppermute(payload, 'x', [(x, (x + dx) % RING) for x in range(RING)])  19.3 us
    pallas_call x1, Pallas kernels, ghost_near(): pl.pallas_call(ghost_kernel, out_shape=jax.ShapeDtypeStruct(start.shape,...  12.8 us
    all_to_all x1, starting transfers between devices, body(): lax.all_to_all(packed, AXES, split_axis=0, concat_axis=0, tiled=True)  11.9 us
    all_to_all x1, starting transfers between devices, body(): lax.all_to_all(payload, AXES[1:], split_axis=0, concat_axis=0, tiled=True)  6 us
    pallas_call x1, Pallas kernels, finish(): pl.pallas_call(functools.partial(finish_kernel, scales=scales), out_shape...  5.7 us
    pallas_call x1, Pallas kernels, parent_payload(): pl.pallas_call(moments_kernel, out_shape=jax.ShapeDtypeStruct((80, 128),...  4.49 us
  transfers between devices with their start and end apart: 5, of which 5 were waited for; matrix products, arithmetic and copies ran while one was open for 0% of the time, Pallas kernels for 39%

profile of v7, /device:TPU:1, one launch (start us, length us, event | category | flops | bytes accessed | tf_op | source)
XLA Modules:
  0.0 121.1 jit_solution(11156378310285779904)
XLA Ops:
  0.0 3.7 %pack.1 = bf16[128,152,128]{2,1,0:T(8,128)(2,1)} custom-call(s32[4,128]{1,0:T(4,128)} %bitcast.10, bf16[3,64,256]{2,1,0:T(8,128)(2,1)} %bitcast.6, bf16[64,16,256]{2,1,0:T(8,128)(2,1)} %charges.3), custom_call_target="tpu_custom_call" | custom-call | bytes 6291456 | tf_op jit(solution)/shard_map/pack/pallas_call | solution.py:111
  3.7 0.0 copy-start.1
  3.7 11.9 %all-to-all-start = ((bf16[128,152,128]{2,1,0:T(8,128)(2,1)}), bf16[128,152,128]{2,1,0:T(8,128)(2,1)}, u32[]{:S(2)}, u32[]{:S(2)}) async-start(bf16[128,152,128]{2,1,0:T(8,128)(2,1)} %pack.1), calls=%async_computation | async-start | bytes 9961472 | tf_op jit(solution)/shard_map/all_to_all | solution.py:579
  15.6 4.5 %moments.1.refs_0_ = bf16[80,128]{1,0:T(8,128)(2,1)} custom-call(bf16[64,16,256]{2,1,0:T(8,128)(2,1)} %charges.3, bf16[64,64,256]{2,1,0:T(8,128)(2,1)} %basis_hbm.1, bf16[64,64,64]{2,1,0:T(8,128)(2,1)} %transfer_hbm.1, bf16[3,8,64]{2,1,0:T(8,128)(2,1)} %bitcast.8), custom_call_target="tpu_custom_call" | custom-call | flops 100000000 | bytes 4194304 | tf_op jit(solution)/shard_map/moments/pallas_call | solution.py:162
  20.1 2.6 %collective-permute-start.2 = (bf16[80,128]{1,0:T(8,128)(2,1)}, bf16[80,128]{1,0:T(8,128)(2,1)S(1)}, u32[]{:S(2)}, u32[]{:S(2)}) collective-permute-start(bf16[80,128]{1,0:T(8,128)(2,1)} %moments.1.refs_0_), channel_id=1, source_target_pairs={{0,96},{32,0},{64,32},{96,64},{1,97},{33,1},{65,33},{97,65},{2,98}... | collective-permute-start | bytes 61448 | tf_op jit(solution)/shard_map/ppermute | solution.py:186
  22.7 0.6 collective-permute-start.1
  23.3 0.6 collective-permute-start
  23.9 0.0 copy-done.1
  23.9 0.6 and_or_fusion.far
  24.5 0.0 copy-start
  24.5 28.4 %local_near.1 = (bf16[64,3,128,256]{3,2,1,0:T(8,128)(2,1)}, s32[1056]{0:T(1024)}, s32[65]{0:T(128)}, f32[64,16,256]{2,1,0:T(8,128)}) custom-call(s32[16,64]{1,0:T(8,128)} %bitcast.11, s32[64]{0:T(128)} %counts.1, bf16[3,64,256]{2,1,0:T(8,128)(2,1)} %bitcast.7, bf16[64,16,256]{2,1,0:T(8,128)(2,1)} %charges.3), custom_call_target="tpu_custom_call" | custom-call | flops 2000000000 | bytes 15728640 | tf_op jit(solution)/shard_map/local_near/pallas_call | solution.py:290
  52.9 17.7 %collective-permute-done.2.refs_3_ = bf16[80,128]{1,0:T(8,128)(2,1)S(1)} collective-permute-done((bf16[80,128]{1,0:T(8,128)(2,1)}, bf16[80,128]{1,0:T(8,128)(2,1)S(1)}, u32[]{:S(2)}, u32[]{:S(2)}) %collective-permute-start.2) | collective-permute-done | bytes 20512 | tf_op jit(solution)/shard_map/ppermute | solution.py:186
  70.6 1.5 %collective-permute-done.1.refs_2_ = bf16[80,128]{1,0:T(8,128)(2,1)S(1)} collective-permute-done((bf16[80,128]{1,0:T(8,128)(2,1)}, bf16[80,128]{1,0:T(8,128)(2,1)S(1)}, u32[]{:S(2)}, u32[]{:S(2)}) %collective-permute-start.1) | collective-permute-done | bytes 20512 | tf_op jit(solution)/shard_map/ppermute | solution.py:186
  72.1 0.1 collective-permute-done.refs_1_
  72.2 0.0 copy-done
  72.2 1.8 %ring_copies.1 = bf16[32,304,128]{2,1,0:T(8,128)(2,1)} custom-call(bf16[80,128]{1,0:T(8,128)(2,1)S(1)} %copy-done, bf16[80,128]{1,0:T(8,128)(2,1)S(1)} %collective-permute-done.refs_1_, bf16[80,128]{1,0:T(8,128)(2,1)S(1)} %collective-permute-done.1.refs_2_, bf16[80,128]{1,0:T(8,128)(2,1)S(1)} %collective-permute-done.2.refs_3_), custom_call_target="tpu_custom_call" | custom-call | bytes 3145728 | tf_op jit(solution)/shard_map/ring_copies/pallas_call | solution.py:188
  74.0 2.8 %all-to-all-done.ghosts_hbm = bf16[128,152,128]{2,1,0:T(8,128)(2,1)} async-done(((bf16[128,152,128]{2,1,0:T(8,128)(2,1)}), bf16[128,152,128]{2,1,0:T(8,128)(2,1)}, u32[]{:S(2)}, u32[]{:S(2)}) %all-to-all-start) | async-done | bytes 4980768 | tf_op jit(solution)/shard_map/all_to_all | solution.py:579
  76.7 6.0 %all-to-all-start.1 = ((bf16[32,304,128]{2,1,0:T(8,128)(2,1)}), bf16[32,304,128]{2,1,0:T(8,128)(2,1)}, u32[]{:S(2)}, u32[]{:S(2)}) async-start(bf16[32,304,128]{2,1,0:T(8,128)(2,1)} %ring_copies.1), calls=%async_computation.1 | async-start | bytes 4980736 | tf_op jit(solution)/shard_map/all_to_all | solution.py:586
  82.7 12.8 %ghost_near.1.near_hbm = f32[64,16,256]{2,1,0:T(8,128)} custom-call(s32[1056]{0:T(1024)} %get-tuple-element.16.items_hbm, s32[65]{0:T(128)} %get-tuple-element.17.starts_hbm, bf16[128,152,128]{2,1,0:T(8,128)(2,1)} %all-to-all-done.ghosts_hbm, bf16[64,3,128,256]{3,2,1,0:T(8,128)(2,1)} %get-tuple-element.19.targets_hbm, f32[64,16,256]{2,1,0:T(8,128)} %get-tuple-element.20.start_hbm), custom_call_target="tpu_custom_call" | custom-call | flops 10000000000 | bytes 20971520 | tf_op jit(solution)/shard_map/ghost_near/pallas_call | solution.py:403
  95.6 19.8 %all-to-all-done.1.parents = bf16[32,304,128]{2,1,0:T(8,128)(2,1)} async-done(((bf16[32,304,128]{2,1,0:T(8,128)(2,1)}), bf16[32,304,128]{2,1,0:T(8,128)(2,1)}, u32[]{:S(2)}, u32[]{:S(2)}) %all-to-all-start.1) | async-done | bytes 2490400 | tf_op jit(solution)/shard_map/all_to_all | solution.py:586
  115.4 5.7 %finish.1 = bf16[64,16,256]{2,1,0:T(8,128)(2,1)} custom-call(s32[8,27]{1,0:T(8,128)} %and_or_fusion.far, bf16[32,304,128]{2,1,0:T(8,128)(2,1)} %all-to-all-done.1.parents, bf16[3,8,64]{2,1,0:T(8,128)(2,1)} %bitcast.9, bf16[64,64,64]{2,1,0:T(8,128)(2,1)} %transfer_hbm.1, bf16[64,64,256]{2,1,0:T(8,128)(2,1)} %basis_hbm.1, f32[64,16,256]{2,1,0:T(8,128)} %ghost_near.1.near_hbm), custom_call_target="tpu_custom_call" | custom-call | flops 100000000 | bytes 8388608 | tf_op jit(solution)/shard_map/finish/pallas_call | solution.py:535
Async XLA Ops:
  3.7 20.2 %copy-start.1 = (s32[8,27]{1,0:T(8,128)S(1)}, s32[8,27]{1,0:T(8,128)}, u32[]{:S(2)}) copy-start(s32[8,27]{1,0:T(8,128)} %param.17) | copy-start | bytes 2596
  3.7 73.0 %all-to-all-start = ((bf16[128,152,128]{2,1,0:T(8,128)(2,1)}), bf16[128,152,128]{2,1,0:T(8,128)(2,1)}, u32[]{:S(2)}, u32[]{:S(2)}) async-start(bf16[128,152,128]{2,1,0:T(8,128)(2,1)} %pack.1), calls=%async_computation | async-start | bytes 9961472 | tf_op jit(solution)/shard_map/all_to_all | solution.py:579
  20.1 50.5 %collective-permute-start.2 = (bf16[80,128]{1,0:T(8,128)(2,1)}, bf16[80,128]{1,0:T(8,128)(2,1)S(1)}, u32[]{:S(2)}, u32[]{:S(2)}) collective-permute-start(bf16[80,128]{1,0:T(8,128)(2,1)} %moments.1.refs_0_), channel_id=1, source_target_pairs={{0,96},{32,0},{64,32},{96,64},{1,97},{33,1},{65,33},{97,65},{2,98}... | collective-permute-start | bytes 61448 | tf_op jit(solution)/shard_map/ppermute | solution.py:186
  22.7 49.4 %collective-permute-start.1 = (bf16[80,128]{1,0:T(8,128)(2,1)}, bf16[80,128]{1,0:T(8,128)(2,1)S(1)}, u32[]{:S(2)}, u32[]{:S(2)}) collective-permute-start(bf16[80,128]{1,0:T(8,128)(2,1)} %moments.1.refs_0_), channel_id=1, source_target_pairs={{0,64},{32,96},{64,0},{96,32},{1,65},{33,97},{65,1},{97,33},{2,66}... | collective-permute-start | bytes 61448 | tf_op jit(solution)/shard_map/ppermute | solution.py:186
  23.3 48.9 %collective-permute-start = (bf16[80,128]{1,0:T(8,128)(2,1)}, bf16[80,128]{1,0:T(8,128)(2,1)S(1)}, u32[]{:S(2)}, u32[]{:S(2)}) collective-permute-start(bf16[80,128]{1,0:T(8,128)(2,1)} %moments.1.refs_0_), channel_id=1, source_target_pairs={{0,32},{32,64},{64,96},{96,0},{1,33},{33,65},{65,97},{97,1},{2,34}... | collective-permute-start | bytes 61448 | tf_op jit(solution)/shard_map/ppermute | solution.py:186
  24.5 47.7 %copy-start = (bf16[80,128]{1,0:T(8,128)(2,1)S(1)}, bf16[80,128]{1,0:T(8,128)(2,1)}, u32[]{:S(2)}) copy-start(bf16[80,128]{1,0:T(8,128)(2,1)} %moments.1.refs_0_) | copy-start | bytes 61444
  76.7 38.7 %all-to-all-start.1 = ((bf16[32,304,128]{2,1,0:T(8,128)(2,1)}), bf16[32,304,128]{2,1,0:T(8,128)(2,1)}, u32[]{:S(2)}, u32[]{:S(2)}) async-start(bf16[32,304,128]{2,1,0:T(8,128)(2,1)} %ring_copies.1), calls=%async_computation.1 | async-start | bytes 4980736 | tf_op jit(solution)/shard_map/all_to_all | solution.py:586
